TPU v7x, 256 devices: a whole 4x4x8 slice. The times are simulated.
256 devices in a mesh: grp: 16 (over x_lo, z), dom: 16 (over y, x_hi, core).
Axes of the slice: x: 4 (x_hi: 2, x_lo: 2; x = x_hi * 2 + x_lo), y: 4, z: 8, core: 2. Of those that a mesh axis runs over, the one named last changes fastest.
Arguments:
- features: bfloat16 [16, 16, 512, 128], P('grp', 'dom'), may hold values from -6 to 6
- w_self: bfloat16 [128, 128], replicated, may hold values from -0.5 to 0.5
- w_neigh: bfloat16 [128, 128], replicated, may hold values from -0.5 to 0.5
- out_bias: float32 [128], replicated, may hold values from -1 to 1
- adj_tiles: bfloat16 [16, 16, 16, 8, 128, 128], P('grp', 'dom')
- tile_rows: int32 [16, 16, 16, 8], P('grp', 'dom'), may hold values from 0 to 3
- tile_cols: int32 [16, 16, 16, 8], P('grp', 'dom'), may hold values from 0 to 3
- tile_count: int32 [16, 16, 16], P('grp', 'dom'), may hold values from 1 to 8, as said below
- send_rows: int32 [16, 16, 16, 256], P('grp', 'dom'), may hold values from 0 to 511
- send_count: int32 [16, 16, 16], P('grp', 'dom'), may hold values from 1 to 256, as said below
- halo_weight: float32 [16, 16, 16, 256], P('grp', 'dom'), may hold values from 0.5 to 2
- recv_rows: int32 [16, 16, 16, 256], P('grp', 'dom'), may hold values from 0 to 511
- cotangent: bfloat16 [16, 16, 512, 128], P('grp', 'dom'), may hold values from -6 to 6
Outputs:
- output: bfloat16 [16, 16, 512, 128], P('grp', 'dom')
- grad_weights: float32 [256, 128], P('grp', 'dom')
- grad_bias: float32 [128], replicated
Inputs may be any that keep to these rules, and one draw needn't show every extreme that they name: tile_count[g, d, g] is 8 for every block; other counts vary from partition to partition. `send_count`: in every node-block group one partition receives 256 used slots from every other partition.
All inputs are finite; a program needn't handle non-finite values.
Results may differ from a plain program's by a relative error of at most 0.0095.
Values may be sent and summed in bfloat16 or wider, within the bound.
A program may use at most 64 MiB of HBM per device.

v0:
```python
import math

import jax
import jax.numpy as jnp
from jax import lax
from jax.sharding import PartitionSpec as P


def passed_along(value, axis, steps):
    count = lax.axis_size(axis)
    pairs = [(source, (source + steps) % count) for source in range(count)]
    return lax.ppermute(value, axis, pairs)


def local(
    features,
    w_self,
    w_neigh,
    out_bias,
    adj_tiles,
    tile_rows,
    tile_cols,
    tile_count,
    send_rows,
    send_count,
    halo_weight,
    recv_rows,
    cotangent,
):
    own_rows = features[0, 0]
    rows_dev, width_in = own_rows.shape
    tile_size = adj_tiles.shape[-1]
    row_tiles = rows_dev // tile_size
    groups = lax.axis_size("grp")
    domains = lax.axis_size("dom")
    grp_index = lax.axis_index("grp")
    dom_index = lax.axis_index("dom")
    highest = lax.Precision.HIGHEST
    tiles_here = adj_tiles[0, 0]
    rows_here = tile_rows[0, 0]
    cols_here = tile_cols[0, 0]
    count_here = tile_count[0, 0]
    slots = rows_here.shape[-1]
    slot_ids = jnp.arange(slots, dtype=jnp.int32)
    tile_ids = jnp.arange(row_tiles, dtype=jnp.int32)
    placing_all = (
        (rows_here[None] == tile_ids[:, None, None])
        & (slot_ids[None, None, :] < count_here[None, :, None])
    ).astype(jnp.float32)

    def absorb(total, panel, source):
        panel_tiles = panel.reshape(row_tiles, tile_size, width_in)
        columns = lax.dynamic_index_in_dim(cols_here, source, 0, keepdims=False)
        targets = lax.dynamic_index_in_dim(rows_here, source, 0, keepdims=False)
        used = lax.dynamic_index_in_dim(count_here, source, 0, keepdims=False)
        weights = lax.dynamic_index_in_dim(tiles_here, source, 0, keepdims=False)
        picked = panel_tiles[columns]
        product = jnp.einsum("sij,sjf->sif", weights, picked, preferred_element_type=jnp.float32)
        placing = ((targets[None, :] == tile_ids[:, None]) & (slot_ids[None, :] < used)).astype(
            jnp.float32
        )
        return total + jnp.einsum("rs,sif->rif", placing, product, precision=highest)

    total = absorb(jnp.zeros((row_tiles, tile_size, width_in), jnp.float32), own_rows, grp_index)

    def advance(turn, carry):
        panel, running = carry
        panel = passed_along(panel, "grp", 1)
        return (panel, absorb(running, panel, jnp.mod(grp_index - turn, groups)))

    _, total = lax.fori_loop(1, groups, advance, (own_rows, total))
    local_sum = total.reshape(rows_dev, width_in)
    row_weight = jnp.sum(tiles_here, axis=-1, dtype=jnp.float32)
    local_degree = jnp.einsum("rbs,bsi->ri", placing_all, row_weight, precision=highest).reshape(
        rows_dev
    )
    send_index = send_rows[0, 0]
    halo_slots = send_index.shape[-1]
    halo_ids = jnp.arange(halo_slots, dtype=jnp.int32)
    dom_ids = jnp.arange(domains, dtype=jnp.int32)
    picked_rows = own_rows[send_index]
    keep = (halo_ids[None, :] < send_count[0, 0][:, None]) & (dom_ids[:, None] != dom_index)
    edge_weight = jnp.where(keep, halo_weight[0, 0], 0.0)
    outgoing = (edge_weight[..., None] * picked_rows).astype(jnp.bfloat16)
    arrived, arrived_weight = (
        lax.all_to_all(outgoing, "dom", split_axis=0, concat_axis=0, tiled=True),
        lax.all_to_all(
            edge_weight.astype(jnp.bfloat16), "dom", split_axis=0, concat_axis=0, tiled=True
        ).astype(edge_weight.dtype),
    )
    landing = recv_rows[0, 0].reshape(-1)
    position = jnp.arange(rows_dev, dtype=jnp.int32)
    hits = landing[None, :] == position[:, None]
    halo_sum = jnp.dot(
        hits.astype(jnp.bfloat16), arrived.reshape(-1, width_in), preferred_element_type=jnp.float32
    )
    halo_degree = jnp.sum(jnp.where(hits, arrived_weight.reshape(-1)[None, :], 0.0), axis=1)
    aggregate = (
        (local_sum + halo_sum) / jnp.sqrt(1.0 + local_degree + halo_degree)[:, None]
    ).astype(jnp.bfloat16)
    preact = (
        jnp.dot(own_rows, w_self, preferred_element_type=jnp.float32)
        + jnp.dot(aggregate, w_neigh, preferred_element_type=jnp.float32)
        + out_bias
    )
    sigma = jax.nn.sigmoid(preact)
    output = (preact * sigma).astype(jnp.bfloat16)
    slope = (cotangent[0, 0].astype(jnp.float32) * sigma * (1.0 + preact * (1.0 - sigma))).astype(
        jnp.bfloat16
    )
    term_w = jnp.concatenate(
        [
            jnp.einsum("nf,nh->fh", own_rows, slope, preferred_element_type=jnp.float32),
            jnp.einsum("nf,nh->fh", aggregate, slope, preferred_element_type=jnp.float32),
        ],
        axis=0,
    )
    term_b = jnp.sum(slope.astype(jnp.float32), axis=0)
    units = term_w.shape[1]
    rows_share = term_w.shape[0] // groups
    cols_share = units // domains
    total_w, total_b = lax.psum((term_w, term_b), ("grp", "dom"))
    block_w = lax.dynamic_slice(
        total_w, (grp_index * rows_share, dom_index * cols_share), (rows_share, cols_share)
    )
    scale = 1.0 / math.sqrt(rows_dev * groups * domains)
    return (output.reshape(1, 1, rows_dev, units), scale * block_w, scale * total_b)


def solution(mesh):
    placed = (
        P("grp", "dom", None, None),
        P(),
        P(),
        P(),
        P("grp", "dom", None, None, None, None),
        P("grp", "dom", None, None),
        P("grp", "dom", None, None),
        P("grp", "dom", None),
        P("grp", "dom", None, None),
        P("grp", "dom", None),
        P("grp", "dom", None, None),
        P("grp", "dom", None, None),
        P("grp", "dom", None, None),
    )
    return jax.shard_map(
        local,
        mesh=mesh,
        in_specs=placed,
        out_specs=(P("grp", "dom", None, None), P("grp", "dom"), P()),
        check_vma=False,
    )
```

profile of v0, /device:TPU:1, one launch (start us, length us, event | category | flops | bytes accessed | tf_op | source)
XLA Modules:
  0.0 464.7 jit_solution(2160511659275895291)
XLA Ops:
  7.2 0.9 fusion.38
  9.9 8.4 %all-to-all-start.1 = ((bf16[16,2,128]{2,1,0:T(2,128)(2,1)}), bf16[16,2,128]{2,1,0:T(2,128)(2,1)S(1)}, u32[]{:S(2)}, u32[]{:S(2)}) async-start(bf16[16,2,128]{2,1,0:T(2,128)(2,1)} %reshape.350), calls=%async_computation.1 | async-start | bytes 16384 | tf_op jit(solution)/shard_map/all_to_all | solution.py:87
  18.3 0.8 bitcast_select_fusion
  19.1 0.9 dynamic-slice_reduce_fusion
  20.1 1.3 constant_dynamic-slice_fusion.2
  22.1 0.9 copy.43
  25.3 12.1 %gather_fusion.2 = bf16[4096,128]{1,0:T(8,128)(2,1)S(1)} fusion(bf16[512,128]{1,0:T(8,128)(2,1)S(1)} %bitcast.107, s32[4096]{0:T(1024)S(1)} %broadcast_clamp_fusion), kind=kCustom, calls=%fused_computation.2 | custom fusion | bytes 2113536 | tf_op jit(solution)/shard_map/gather | solution.py:81
  38.2 1.2 fusion.32
  39.4 1.5 fusion.19
  41.6 137.8 %while.18 = (s32[]{:T(128)}, bf16[512,128]{1,0:T(8,128)(2,1)S(1)}, f32[4,128,128]{2,0,1:T(4,128)S(1)}, s32[]{:T(128)}, s32[16,8]{1,0:T(8,128)S(1)}, /*index=5*/s...) while((s32[]{:T(128)}, bf16[512,128]{1,0:T(8,128)(2,1)S(1)}, ...), condition=%wide.region_1.2_spmd.clone, body=%wide.region_0.1_spmd.clone.sunk | while | flops 39912560 | bytes 3412548 | solution.py:71
  41.6 1.7 collective-permute-start
  44.7 6.3 %collective-permute-done = bf16[512,128]{1,0:T(8,128)(2,1)S(1)} collective-permute-done((bf16[512,128]{1,0:T(8,128)(2,1)S(1)}, bf16[512,128]{1,0:T(8,128)(2,1)S(1)}, u32[]{:S(2)}, u32[]{:S(2)}) %collective-permute-start) | collective-permute-done | bytes 131104 | tf_op jit(solution)/shard_map/while/body/eval_jaxpr/ppermute | solution.py:12
  51.7 1.2 fusion.77
  52.8 0.9 convolution_add_fusion.3
  55.3 5.0 %collective-permute-done = bf16[512,128]{1,0:T(8,128)(2,1)S(1)} collective-permute-done((bf16[512,128]{1,0:T(8,128)(2,1)S(1)}, bf16[512,128]{1,0:T(8,128)(2,1)S(1)}, u32[]{:S(2)}, u32[]{:S(2)}) %collective-permute-start) | collective-permute-done | bytes 131104 | tf_op jit(solution)/shard_map/while/body/eval_jaxpr/ppermute | solution.py:12
  61.0 1.2 fusion.77
  62.1 0.9 convolution_add_fusion.3
  64.6 4.5 collective-permute-done
  69.7 1.2 fusion.77
  70.9 0.9 convolution_add_fusion.3
  73.4 4.5 collective-permute-done
  78.4 1.2 fusion.77
  79.6 0.9 convolution_add_fusion.3
  82.1 4.5 collective-permute-done
  87.2 1.2 fusion.77
  88.4 0.9 convolution_add_fusion.3
  90.9 4.5 collective-permute-done
  95.9 1.2 fusion.77
  97.1 0.9 convolution_add_fusion.3
  99.6 4.5 collective-permute-done
  104.7 1.2 fusion.77
  105.9 0.9 convolution_add_fusion.3
  108.4 4.5 collective-permute-done
  113.4 1.2 fusion.77
  114.6 0.9 convolution_add_fusion.3
  117.1 4.9 %collective-permute-done = bf16[512,128]{1,0:T(8,128)(2,1)S(1)} collective-permute-done((bf16[512,128]{1,0:T(8,128)(2,1)S(1)}, bf16[512,128]{1,0:T(8,128)(2,1)S(1)}, u32[]{:S(2)}, u32[]{:S(2)}) %collective-permute-start) | collective-permute-done | bytes 131104 | tf_op jit(solution)/shard_map/while/body/eval_jaxpr/ppermute | solution.py:12
  122.6 1.2 fusion.77
  123.8 0.9 convolution_add_fusion.3
  126.3 6.0 %collective-permute-done = bf16[512,128]{1,0:T(8,128)(2,1)S(1)} collective-permute-done((bf16[512,128]{1,0:T(8,128)(2,1)S(1)}, bf16[512,128]{1,0:T(8,128)(2,1)S(1)}, u32[]{:S(2)}, u32[]{:S(2)}) %collective-permute-start) | collective-permute-done | bytes 131104 | tf_op jit(solution)/shard_map/while/body/eval_jaxpr/ppermute | solution.py:12
  132.9 1.2 fusion.77
  134.1 0.9 convolution_add_fusion.3
  136.6 5.1 %collective-permute-done = bf16[512,128]{1,0:T(8,128)(2,1)S(1)} collective-permute-done((bf16[512,128]{1,0:T(8,128)(2,1)S(1)}, bf16[512,128]{1,0:T(8,128)(2,1)S(1)}, u32[]{:S(2)}, u32[]{:S(2)}) %collective-permute-start) | collective-permute-done | bytes 131104 | tf_op jit(solution)/shard_map/while/body/eval_jaxpr/ppermute | solution.py:12
  142.3 1.2 fusion.77
  143.5 0.9 convolution_add_fusion.3
  146.0 4.5 collective-permute-done
  151.0 1.2 fusion.77
  152.2 0.9 convolution_add_fusion.3
  154.7 4.5 collective-permute-done
  159.8 1.2 fusion.77
  161.0 0.9 convolution_add_fusion.3
  163.5 4.5 collective-permute-done
  168.5 1.2 fusion.77
  169.7 0.9 convolution_add_fusion.3
  172.2 4.5 collective-permute-done
  177.3 1.2 fusion.77
  178.5 0.9 convolution_add_fusion.3
  179.5 23.0 %all-to-all-start = ((bf16[16,256,128]{2,1,0:T(8,128)(2,1)}), bf16[16,256,128]{2,1,0:T(8,128)(2,1)S(1)}, u32[]{:S(2)}, u32[]{:S(2)}) async-start(bf16[16,256,128]{2,1,0:T(8,128)(2,1)} %fusion.19), calls=%async_computation | async-start | bytes 2097152 | tf_op jit(solution)/shard_map/all_to_all | solution.py:86
  202.6 3.4 convert_reduce_fusion
  206.1 1.1 select_reduce_fusion
  207.4 12.3 %all-to-all-done = bf16[16,256,128]{2,1,0:T(8,128)(2,1)S(1)} async-done(((bf16[16,256,128]{2,1,0:T(8,128)(2,1)}), bf16[16,256,128]{2,1,0:T(8,128)(2,1)S(1)}, u32[]{:S(2)}, u32[]{:S(2)}) %all-to-all-start) | async-done | bytes 1048608 | tf_op jit(solution)/shard_map/all_to_all | solution.py:86
  219.7 1.6 fusion.23
  221.4 0.9 convert_reduce_fusion.1
  223.5 72.7 %psum.15 = f32[128]{0:T(128)S(1)} all-reduce(f32[128]{0:T(128)S(1)} %get-tuple-element.315), channel_id=1, replica_groups=mesh['grp'=16,'dom'=16] {'grp','dom'}, use_global_device_ids=true, to_apply=%region_6.7 | all-reduce | flops 128 | bytes 1024 | tf_op jit(solution)/shard_map/psum | solution.py:122
  296.8 159.7 %all-reduce.2.cloned.1.call-done = f32[256,128]{1,0:T(8,128)} async-done(((f32[256,128]{1,0:T(8,128)}), f32[256,128]{1,0:T(8,128)}) %all-reduce.2.cloned.1.call-update) | async-done | bytes 131088 | tf_op jit(solution)/shard_map/psum | solution.py:122
  (165 shorter events, 40.8 us)
Async XLA Ops:
  7.2 214.2 %copy-start = (bf16[128,128]{1,0:T(8,128)(2,1)S(1)}, bf16[128,128]{1,0:T(8,128)(2,1)}, u32[]{:S(2)}) copy-start(bf16[128,128]{1,0:T(8,128)(2,1)} %param.17) | copy-start | bytes 98308
  7.2 18.1 %copy-start.1 = (bf16[1,1,512,128]{3,2,1,0:T(8,128)(2,1)S(1)}, bf16[1,1,512,128]{3,2,1,0:T(8,128)(2,1)}, u32[]{:S(2)}) copy-start(bf16[1,1,512,128]{3,2,1,0:T(8,128)(2,1)} %param.15) | copy-start | bytes 393220
  9.9 169.6 %all-to-all-start.1 = ((bf16[16,2,128]{2,1,0:T(2,128)(2,1)}), bf16[16,2,128]{2,1,0:T(2,128)(2,1)S(1)}, u32[]{:S(2)}, u32[]{:S(2)}) async-start(bf16[16,2,128]{2,1,0:T(2,128)(2,1)} %reshape.350), calls=%async_computation.1 | async-start | bytes 16384 | tf_op jit(solution)/shard_map/all_to_all | solution.py:87
  25.3 12.2 %copy-start.3 = (bf16[128,128]{1,0:T(8,128)(2,1)S(1)}, bf16[128,128]{1,0:T(8,128)(2,1)}, u32[]{:S(2)}) copy-start(bf16[128,128]{1,0:T(8,128)(2,1)} %param.16) | copy-start | bytes 98308
  37.4 4.1 copy-start.6
  41.6 137.9 %copy-start.4 = (s32[1,1,16,256]{3,2,1,0:T(8,128)S(1)}, s32[1,1,16,256]{3,2,1,0:T(8,128)}, u32[]{:S(2)}) copy-start(s32[1,1,16,256]{3,2,1,0:T(8,128)} %param.26) | copy-start | bytes 49156
  41.6 9.5 %collective-permute-start = (bf16[512,128]{1,0:T(8,128)(2,1)S(1)}, bf16[512,128]{1,0:T(8,128)(2,1)S(1)}, u32[]{:S(2)}, u32[]{:S(2)}) collective-permute-start(bf16[512,128]{1,0:T(8,128)(2,1)S(1)} %get-tuple-element.382), channel_id=1, source_target_pairs={{0,16},{16,32},{32,48},{48,64},{64,80},{80,96},{96,112},{112,128},... | collective-permute-start | bytes 393224 | tf_op jit(solution)/shard_map/while/body/eval_jaxpr/ppermute | solution.py:12
  53.8 6.5 %collective-permute-start = (bf16[512,128]{1,0:T(8,128)(2,1)S(1)}, bf16[512,128]{1,0:T(8,128)(2,1)S(1)}, u32[]{:S(2)}, u32[]{:S(2)}) collective-permute-start(bf16[512,128]{1,0:T(8,128)(2,1)S(1)} %get-tuple-element.382), channel_id=1, source_target_pairs={{0,16},{16,32},{32,48},{48,64},{64,80},{80,96},{96,112},{112,128},... | collective-permute-start | bytes 393224 | tf_op jit(solution)/shard_map/while/body/eval_jaxpr/ppermute | solution.py:12
  63.1 6.0 %collective-permute-start = (bf16[512,128]{1,0:T(8,128)(2,1)S(1)}, bf16[512,128]{1,0:T(8,128)(2,1)S(1)}, u32[]{:S(2)}, u32[]{:S(2)}) collective-permute-start(bf16[512,128]{1,0:T(8,128)(2,1)S(1)} %get-tuple-element.382), channel_id=1, source_target_pairs={{0,16},{16,32},{32,48},{48,64},{64,80},{80,96},{96,112},{112,128},... | collective-permute-start | bytes 393224 | tf_op jit(solution)/shard_map/while/body/eval_jaxpr/ppermute | solution.py:12
  71.8 6.0 %collective-permute-start = (bf16[512,128]{1,0:T(8,128)(2,1)S(1)}, bf16[512,128]{1,0:T(8,128)(2,1)S(1)}, u32[]{:S(2)}, u32[]{:S(2)}) collective-permute-start(bf16[512,128]{1,0:T(8,128)(2,1)S(1)} %get-tuple-element.382), channel_id=1, source_target_pairs={{0,16},{16,32},{32,48},{48,64},{64,80},{80,96},{96,112},{112,128},... | collective-permute-start | bytes 393224 | tf_op jit(solution)/shard_map/while/body/eval_jaxpr/ppermute | solution.py:12
  80.6 6.0 %collective-permute-start = (bf16[512,128]{1,0:T(8,128)(2,1)S(1)}, bf16[512,128]{1,0:T(8,128)(2,1)S(1)}, u32[]{:S(2)}, u32[]{:S(2)}) collective-permute-start(bf16[512,128]{1,0:T(8,128)(2,1)S(1)} %get-tuple-element.382), channel_id=1, source_target_pairs={{0,16},{16,32},{32,48},{48,64},{64,80},{80,96},{96,112},{112,128},... | collective-permute-start | bytes 393224 | tf_op jit(solution)/shard_map/while/body/eval_jaxpr/ppermute | solution.py:12
  89.3 6.0 %collective-permute-start = (bf16[512,128]{1,0:T(8,128)(2,1)S(1)}, bf16[512,128]{1,0:T(8,128)(2,1)S(1)}, u32[]{:S(2)}, u32[]{:S(2)}) collective-permute-start(bf16[512,128]{1,0:T(8,128)(2,1)S(1)} %get-tuple-element.382), channel_id=1, source_target_pairs={{0,16},{16,32},{32,48},{48,64},{64,80},{80,96},{96,112},{112,128},... | collective-permute-start | bytes 393224 | tf_op jit(solution)/shard_map/while/body/eval_jaxpr/ppermute | solution.py:12
  98.1 6.0 %collective-permute-start = (bf16[512,128]{1,0:T(8,128)(2,1)S(1)}, bf16[512,128]{1,0:T(8,128)(2,1)S(1)}, u32[]{:S(2)}, u32[]{:S(2)}) collective-permute-start(bf16[512,128]{1,0:T(8,128)(2,1)S(1)} %get-tuple-element.382), channel_id=1, source_target_pairs={{0,16},{16,32},{32,48},{48,64},{64,80},{80,96},{96,112},{112,128},... | collective-permute-start | bytes 393224 | tf_op jit(solution)/shard_map/while/body/eval_jaxpr/ppermute | solution.py:12
  106.8 6.0 %collective-permute-start = (bf16[512,128]{1,0:T(8,128)(2,1)S(1)}, bf16[512,128]{1,0:T(8,128)(2,1)S(1)}, u32[]{:S(2)}, u32[]{:S(2)}) collective-permute-start(bf16[512,128]{1,0:T(8,128)(2,1)S(1)} %get-tuple-element.382), channel_id=1, source_target_pairs={{0,16},{16,32},{32,48},{48,64},{64,80},{80,96},{96,112},{112,128},... | collective-permute-start | bytes 393224 | tf_op jit(solution)/shard_map/while/body/eval_jaxpr/ppermute | solution.py:12
  115.6 6.4 %collective-permute-start = (bf16[512,128]{1,0:T(8,128)(2,1)S(1)}, bf16[512,128]{1,0:T(8,128)(2,1)S(1)}, u32[]{:S(2)}, u32[]{:S(2)}) collective-permute-start(bf16[512,128]{1,0:T(8,128)(2,1)S(1)} %get-tuple-element.382), channel_id=1, source_target_pairs={{0,16},{16,32},{32,48},{48,64},{64,80},{80,96},{96,112},{112,128},... | collective-permute-start | bytes 393224 | tf_op jit(solution)/shard_map/while/body/eval_jaxpr/ppermute | solution.py:12
  124.7 7.5 %collective-permute-start = (bf16[512,128]{1,0:T(8,128)(2,1)S(1)}, bf16[512,128]{1,0:T(8,128)(2,1)S(1)}, u32[]{:S(2)}, u32[]{:S(2)}) collective-permute-start(bf16[512,128]{1,0:T(8,128)(2,1)S(1)} %get-tuple-element.382), channel_id=1, source_target_pairs={{0,16},{16,32},{32,48},{48,64},{64,80},{80,96},{96,112},{112,128},... | collective-permute-start | bytes 393224 | tf_op jit(solution)/shard_map/while/body/eval_jaxpr/ppermute | solution.py:12
  135.0 6.7 %collective-permute-start = (bf16[512,128]{1,0:T(8,128)(2,1)S(1)}, bf16[512,128]{1,0:T(8,128)(2,1)S(1)}, u32[]{:S(2)}, u32[]{:S(2)}) collective-permute-start(bf16[512,128]{1,0:T(8,128)(2,1)S(1)} %get-tuple-element.382), channel_id=1, source_target_pairs={{0,16},{16,32},{32,48},{48,64},{64,80},{80,96},{96,112},{112,128},... | collective-permute-start | bytes 393224 | tf_op jit(solution)/shard_map/while/body/eval_jaxpr/ppermute | solution.py:12
  144.4 6.0 %collective-permute-start = (bf16[512,128]{1,0:T(8,128)(2,1)S(1)}, bf16[512,128]{1,0:T(8,128)(2,1)S(1)}, u32[]{:S(2)}, u32[]{:S(2)}) collective-permute-start(bf16[512,128]{1,0:T(8,128)(2,1)S(1)} %get-tuple-element.382), channel_id=1, source_target_pairs={{0,16},{16,32},{32,48},{48,64},{64,80},{80,96},{96,112},{112,128},... | collective-permute-start | bytes 393224 | tf_op jit(solution)/shard_map/while/body/eval_jaxpr/ppermute | solution.py:12
  153.2 6.0 %collective-permute-start = (bf16[512,128]{1,0:T(8,128)(2,1)S(1)}, bf16[512,128]{1,0:T(8,128)(2,1)S(1)}, u32[]{:S(2)}, u32[]{:S(2)}) collective-permute-start(bf16[512,128]{1,0:T(8,128)(2,1)S(1)} %get-tuple-element.382), channel_id=1, source_target_pairs={{0,16},{16,32},{32,48},{48,64},{64,80},{80,96},{96,112},{112,128},... | collective-permute-start | bytes 393224 | tf_op jit(solution)/shard_map/while/body/eval_jaxpr/ppermute | solution.py:12
  161.9 6.0 %collective-permute-start = (bf16[512,128]{1,0:T(8,128)(2,1)S(1)}, bf16[512,128]{1,0:T(8,128)(2,1)S(1)}, u32[]{:S(2)}, u32[]{:S(2)}) collective-permute-start(bf16[512,128]{1,0:T(8,128)(2,1)S(1)} %get-tuple-element.382), channel_id=1, source_target_pairs={{0,16},{16,32},{32,48},{48,64},{64,80},{80,96},{96,112},{112,128},... | collective-permute-start | bytes 393224 | tf_op jit(solution)/shard_map/while/body/eval_jaxpr/ppermute | solution.py:12
  170.7 6.0 %collective-permute-start = (bf16[512,128]{1,0:T(8,128)(2,1)S(1)}, bf16[512,128]{1,0:T(8,128)(2,1)S(1)}, u32[]{:S(2)}, u32[]{:S(2)}) collective-permute-start(bf16[512,128]{1,0:T(8,128)(2,1)S(1)} %get-tuple-element.382), channel_id=1, source_target_pairs={{0,16},{16,32},{32,48},{48,64},{64,80},{80,96},{96,112},{112,128},... | collective-permute-start | bytes 393224 | tf_op jit(solution)/shard_map/while/body/eval_jaxpr/ppermute | solution.py:12
  179.4 27.8 %copy-start.2 = (s32[1,1,16,8]{2,3,1,0:T(8,128)S(1)}, s32[1,1,16,8]{2,3,1,0:T(8,128)}, u32[]{:S(2)}) copy-start(s32[1,1,16,8]{2,3,1,0:T(8,128)} %param.20) | copy-start | bytes 1540
  179.5 40.2 %all-to-all-start = ((bf16[16,256,128]{2,1,0:T(8,128)(2,1)}), bf16[16,256,128]{2,1,0:T(8,128)(2,1)S(1)}, u32[]{:S(2)}, u32[]{:S(2)}) async-start(bf16[16,256,128]{2,1,0:T(8,128)(2,1)} %fusion.19), calls=%async_computation | async-start | bytes 2097152 | tf_op jit(solution)/shard_map/all_to_all | solution.py:86
  202.5 253.9 %all-reduce.2.cloned.1.call-start = ((), (), s32[]{:S(2)}) async-start(), calls=%async_computation.2 | async-start | bytes 262144 | tf_op jit(solution)/shard_map/psum | solution.py:122
  202.6 18.8 %copy-start.5 = (bf16[1,1,512,128]{3,2,1,0:T(8,128)(2,1)S(1)}, bf16[1,1,512,128]{3,2,1,0:T(8,128)(2,1)}, u32[]{:S(2)}) copy-start(bf16[1,1,512,128]{3,2,1,0:T(8,128)(2,1)} %param.27) | copy-start | bytes 393220
  202.6 18.8 %copy-start.7 = (f32[128]{0:T(128)S(1)}, f32[128]{0:T(128)}, u32[]{:S(2)}) copy-start(f32[128]{0:T(128)} %param.18) | copy-start | bytes 1540
Sparse Core Ops, SparseCore 0:
  223.6 232.7 all-reduce.1
where the time goes:
time: 466 us; the launch traced here: 465 us
  waiting for transfers between devices  244 us (52%)
  blocking collectives  72.7 us (16%)
  local copies, waits for them, and re-layouts  38.5 us (8%)
  matrix products  36.8 us (8%)
  starting transfers between devices  34.4 us (7%)
  other arithmetic  22.5 us (5%)
  between operations  14.3 us (3%)
    psum x1, waiting for transfers between devices, local(): total_w, total_b = lax.psum((term_w, term_b), ('grp', 'dom'))  160 us
    psum x1, blocking collectives, local(): total_w, total_b = lax.psum((term_w, term_b), ('grp', 'dom'))  72.7 us
    ppermute x15, waiting for transfers between devices, passed_along(): return lax.ppermute(value, axis, pairs)  72.1 us
    all_to_all x1, starting transfers between devices, local(): lax.all_to_all(outgoing, 'dom', split_axis=0, concat_axis=0, tiled=True)  23 us
    dot_general x16, matrix products, absorb(): jnp.einsum('sij,sjf->sif', weights, picked, preferred_element_type=jnp.fl...  18.7 us
    dot_general x16, matrix products, absorb(): jnp.einsum('rs,sif->rif', placing, product, precision=highest)  14.6 us
    all_to_all x1, waiting for transfers between devices, local(): lax.all_to_all(outgoing, 'dom', split_axis=0, concat_axis=0, tiled=True)  12.3 us
    gather x1, local copies, waits for them, and re-layouts, local(): picked_rows = own_rows[send_index]  12.1 us
  transfers between devices with their start and end apart: 18, of which 17 were waited for; matrix products, arithmetic and copies ran while one was open for 19% of the time, Pallas kernels for 0%

commit v1 on v0

v1 whole, which is shorter than its diff:
```python
import math

import jax
import jax.numpy as jnp
from jax import lax
from jax.experimental import pallas as pl
from jax.experimental.pallas import tpu as pltpu
from jax.sharding import PartitionSpec as P

MESH = pl.DeviceIdType.MESH
ROWS, FEATS, TILE, SLOTS, HALO = 512, 128, 128, 8, 256
HALF = ROWS // 2
NZ = 8
PAY = FEATS + 16
BF16, F32 = jnp.bfloat16, jnp.float32


def kernel(
    feat, adj, cot, wself, wneigh, bias, trows, tcols, tcount, srows, scount, hweight, rrows,
    out, gw, gb,
    part, adjv, cotv, stage, xcat, acc, xt, hsend, hrecv, prhs, outv, catv, tbuf, rec1, tb2, rec2, tposed,
    lsem, asend, arecv, hss, hrs, p1s, p1r, p2s, p2r,
):
    g, d = lax.axis_index("grp"), lax.axis_index("dom")
    xl, z = g // NZ, lax.rem(g, NZ)
    y, xh, core = d // 4, lax.rem(d // 2, 2), lax.rem(d, 2)
    up = xl * NZ + lax.rem(z + 1, NZ)
    down = xl * NZ + lax.rem(z + NZ - 1, NZ)
    side = (1 - xl) * NZ + z

    def dom_to(j):
        dy, dx, dc = j // 4, lax.rem(j // 2, 2), lax.rem(j, 2)
        return lax.rem(y + dy, 4) * 4 + lax.rem(xh + dx, 2) * 2 + lax.rem(core + dc, 2)

    def dom_from(j):
        dy, dx, dc = j // 4, lax.rem(j // 2, 2), lax.rem(j, 2)
        return lax.rem(y + 4 - dy, 4) * 4 + lax.rem(xh + dx, 2) * 2 + lax.rem(core + dc, 2)

    def grp_to(j):
        dx, dz = j // NZ, lax.rem(j, NZ)
        return lax.rem(xl + dx, 2) * NZ + lax.rem(z + dz, NZ)

    load_x = pltpu.make_async_copy(feat, part.at[0], lsem.at[0])
    load_a = pltpu.make_async_copy(adj, adjv, lsem.at[1])
    load_c = pltpu.make_async_copy(cot, cotv, lsem.at[2])
    load_x.start()
    load_a.start()
    load_c.start()

    barrier = pltpu.get_barrier_semaphore()

    @pl.loop(1, 16)
    def _(j):
        pl.semaphore_signal(barrier, inc=1, device_id=(grp_to(j), d), device_id_type=MESH)
        pl.semaphore_signal(barrier, inc=1, device_id=(g, dom_to(j)), device_id_type=MESH)

    load_x.wait()
    xt[...] = part[0].T
    acc[...] = jnp.zeros_like(acc)
    xcat[:, FEATS:] = jnp.ones((SLOTS * TILE, FEATS), BF16)

    node = lax.broadcasted_iota(jnp.int32, (ROWS, HALO), 0)
    lane = lax.broadcasted_iota(jnp.int32, (1, HALO), 1)

    def build_halo(j):
        to = dom_to(j)
        pick = jnp.where(node == srows[pl.ds(to, 1), :], 1.0, 0.0).astype(BF16)
        weight = jnp.where(lane < scount[0, to], hweight[pl.ds(to, 1), :], 0.0)
        rows = jnp.dot(xt[...], pick, preferred_element_type=F32)
        hsend[j, 0:FEATS, :] = (rows * weight).astype(BF16)
        hsend[j, FEATS:PAY, :] = jnp.broadcast_to(weight, (PAY - FEATS, HALO)).astype(BF16)

    def halo_copy(j):
        return pltpu.make_async_remote_copy(
            src_ref=hsend.at[j], dst_ref=hrecv.at[j], send_sem=hss.at[j], recv_sem=hrs.at[j],
            device_id=(g, dom_to(j)), device_id_type=MESH,
        )

    sent = []

    def send(slot_from, slot_to, h, to):
        n = len(sent)
        copy = pltpu.make_async_remote_copy(
            src_ref=part.at[slot_from, pl.ds(h * HALF, HALF), :],
            dst_ref=part.at[slot_to, pl.ds(h * HALF, HALF), :],
            send_sem=asend.at[n], recv_sem=arecv.at[2 * slot_to + h],
            device_id=(to, d), device_id_type=MESH,
        )
        copy.start()
        sent.append(copy)

    def landed(slot, h):
        pltpu.make_async_remote_copy(
            src_ref=part.at[slot, pl.ds(h * HALF, HALF), :],
            dst_ref=part.at[slot, pl.ds(h * HALF, HALF), :],
            send_sem=asend.at[0], recv_sem=arecv.at[2 * slot + h],
            device_id=(up, d), device_id_type=MESH,
        ).wait_recv()

    def absorb(slot, source):
        stage[...] = part[slot].reshape(4, TILE, FEATS)
        for s in range(SLOTS):
            xcat[s * TILE:(s + 1) * TILE, 0:FEATS] = stage[tcols[source, s]]
        limit = jnp.full((16, TILE), tcount[0, source], jnp.int32)
        for r in range(4):
            kept = []
            for s in range(SLOTS):
                target = jnp.full((16, TILE), trows[source, s], jnp.int32)
                on = jnp.where((target == r) & (limit > s), 1.0, 0.0).astype(BF16)
                kept.append(adjv[source, s] * jnp.concatenate([on] * (TILE // 16), axis=0))
            acc[r * TILE:(r + 1) * TILE, :] += jnp.dot(
                jnp.concatenate(kept, axis=1), xcat[...], preferred_element_type=F32
            )

    def absorb_step(first, count, dist):
        def body(k, _):
            source = lax.rem(xl + k // 2, 2) * NZ + lax.rem(z + NZ + dist * (2 * lax.rem(k, 2) - 1), NZ)
            absorb(first + k, source)
            return 0
        lax.fori_loop(0, count, body, 0)

    def take_halo(lo, hi):
        def body(j, _):
            halo_copy(j).wait_recv()
            source = dom_from(j)
            prhs[0:FEATS, :] = hrecv[j, 0:FEATS, :]
            weights = hrecv[j, FEATS:PAY, :]
            for i in range(FEATS // 16):
                prhs[FEATS + 16 * i:FEATS + 16 * (i + 1), :] = weights
            hits = jnp.where(node == rrows[pl.ds(source, 1), :], 1.0, 0.0).astype(BF16)
            acc[...] += lax.dot_general(
                hits, prhs[...], (((1,), (1,)), ((), ())), preferred_element_type=F32
            )
            return 0
        lax.fori_loop(lo, hi, body, 0)

    pl.semaphore_wait(barrier, 30)

    send(0, 1, 1, side)
    send(0, 2, 0, up)
    send(0, 3, 0, down)
    send(0, 2, 1, up)
    send(0, 3, 1, down)
    send(0, 1, 0, side)

    @pl.loop(1, 16)
    def _(j):
        build_halo(j)
        halo_copy(j).start()

    landed(1, 1)
    send(1, 4, 1, up)
    send(1, 5, 1, down)
    load_a.wait()
    for dist in (1, 2):
        a = 4 * dist - 2
        landed(a, 0)
        send(a, a + 4, 0, up)
        send(a, a + 2, 0, side)
        landed(a + 1, 0)
        send(a + 1, a + 5, 0, down)
        send(a + 1, a + 3, 0, side)
        landed(a, 1)
        send(a, a + 4, 1, up)
        landed(a + 1, 1)
        send(a + 1, a + 5, 1, down)
        landed(a + 2, 1)
        send(a + 2, a + 6, 1, up)
        landed(a + 3, 1)
        send(a + 3, a + 7, 1, down)
        if dist == 1:
            landed(1, 0)
            absorb(0, g)
            absorb(1, side)
        else:
            landed(4, 0)
            landed(5, 0)
            absorb_step(2, 4, 1)
    landed(10, 0)
    send(10, 14, 0, up)
    send(10, 12, 0, side)
    landed(11, 0)
    send(11, 13, 0, side)
    landed(10, 1)
    landed(11, 1)
    send(11, 14, 1, down)
    landed(12, 1)
    send(12, 15, 1, up)
    landed(13, 1)
    landed(8, 0)
    landed(9, 0)
    absorb_step(6, 4, 2)
    take_halo(1, 6)
    landed(14, 0)
    send(14, 15, 0, side)
    landed(12, 0)
    landed(13, 0)
    absorb_step(10, 4, 3)
    take_halo(6, 16)
    landed(14, 1)
    landed(15, 1)
    landed(15, 0)
    absorb_step(14, 1, 4)
    absorb(15, lax.rem(xl + 1, 2) * NZ + lax.rem(z + 4, NZ))

    load_c.wait()
    wcat = jnp.concatenate([wself[...], wneigh[...]], axis=0)
    bias_row = bias[...]
    total_b = jnp.zeros((1, FEATS), F32)
    total_w = jnp.zeros((FEATS, 2 * FEATS), F32)
    for r in range(4):
        rs = pl.ds(r * TILE, TILE)
        agg = (acc[rs, 0:FEATS] * lax.rsqrt(1.0 + acc[rs, FEATS:])).astype(BF16)
        cat = jnp.concatenate([part[0, rs, :], agg], axis=1)
        pre = jnp.dot(cat, wcat, preferred_element_type=F32) + bias_row
        sig = jax.nn.sigmoid(pre)
        outv[rs, :] = (pre * sig).astype(BF16)
        slope = (cotv[rs, :].astype(F32) * sig * (1.0 + pre * (1.0 - sig))).astype(BF16)
        total_b += jnp.sum(slope.astype(F32), axis=0, keepdims=True)
        total_w += lax.dot_general(slope, cat, (((0,), (0,)), ((), ())), preferred_element_type=F32)
    store_o = pltpu.make_async_copy(outv, out, lsem.at[3])
    store_o.start()
    tbuf[:, 0:8, :] = total_w[:, 0:FEATS].reshape(16, 8, FEATS)
    tbuf[:, 8:16, :] = total_w[:, FEATS:].reshape(16, 8, FEATS)
    tbuf[:, 16:24, :] = jnp.broadcast_to(total_b[None], (16, 8, FEATS))

    def first_copy(j):
        return pltpu.make_async_remote_copy(
            src_ref=tbuf.at[dom_to(j)], dst_ref=rec1.at[j], send_sem=p1s.at[j], recv_sem=p1r.at[j],
            device_id=(g, dom_to(j)), device_id_type=MESH,
        )

    def second_copy(j):
        return pltpu.make_async_remote_copy(
            src_ref=tb2.at[grp_to(j) // NZ], dst_ref=rec2.at[j], send_sem=p2s.at[j], recv_sem=p2r.at[j],
            device_id=(grp_to(j), d), device_id_type=MESH,
        )

    @pl.loop(1, 16)
    def _(j):
        first_copy(j).start()

    for copy in sent:
        copy.wait_send()

    @pl.loop(1, 16)
    def _(j):
        halo_copy(j).wait_send()

    def add1(j, total):
        first_copy(j).wait_recv()
        return total + rec1[j]

    red = lax.fori_loop(1, 16, add1, tbuf[d])
    tb2[0, 0:8, :] = red[0:8]
    tb2[1, 0:8, :] = red[8:16]
    tb2[0, 8:16, :] = red[16:24]
    tb2[1, 8:16, :] = red[16:24]

    @pl.loop(1, 16)
    def _(j):
        second_copy(j).start()

    def add2(j, total):
        second_copy(j).wait_recv()
        return total + rec2[j]

    fin = lax.fori_loop(1, 16, add2, tb2[xl])
    scale = 1.0 / math.sqrt(ROWS * 256)
    tposed[...] = jnp.transpose(fin[0:8] * scale)
    gw[...] = tposed[pl.ds(pl.multiple_of(z * 16, 16), 16), :]
    gb[...] = fin[8:9] * scale

    @pl.loop(1, 16)
    def _(j):
        first_copy(j).wait_send()
        second_copy(j).wait_send()

    store_o.wait()


def local(
    features, w_self, w_neigh, out_bias, adj_tiles, tile_rows, tile_cols, tile_count, send_rows,
    send_count, halo_weight, recv_rows, cotangent,
):
    vmem = pl.BlockSpec(memory_space=pltpu.VMEM)
    smem = pl.BlockSpec(memory_space=pltpu.SMEM)
    hbm = pl.BlockSpec(memory_space=pl.ANY)
    dma = pltpu.SemaphoreType.DMA
    out, gw, gb = pl.pallas_call(
        kernel,
        out_shape=(
            jax.ShapeDtypeStruct((ROWS, FEATS), BF16),
            jax.ShapeDtypeStruct((16, 8), F32),
            jax.ShapeDtypeStruct((1, FEATS), F32),
        ),
        in_specs=[hbm, hbm, hbm, vmem, vmem, vmem, smem, smem, smem, vmem, smem, vmem, vmem],
        out_specs=(hbm, vmem, vmem),
        scratch_shapes=[
            pltpu.VMEM((16, ROWS, FEATS), BF16),
            pltpu.VMEM((16, SLOTS, TILE, TILE), BF16),
            pltpu.VMEM((ROWS, FEATS), BF16),
            pltpu.VMEM((4, TILE, FEATS), BF16),
            pltpu.VMEM((SLOTS * TILE, 2 * FEATS), BF16),
            pltpu.VMEM((ROWS, 2 * FEATS), F32),
            pltpu.VMEM((FEATS, ROWS), BF16),
            pltpu.VMEM((16, PAY, HALO), BF16),
            pltpu.VMEM((16, PAY, HALO), BF16),
            pltpu.VMEM((2 * FEATS, HALO), BF16),
            pltpu.VMEM((ROWS, FEATS), BF16),
            pltpu.VMEM((ROWS, 2 * FEATS), BF16),
            pltpu.VMEM((16, 24, FEATS), F32),
            pltpu.VMEM((16, 24, FEATS), F32),
            pltpu.VMEM((2, 16, FEATS), F32),
            pltpu.VMEM((16, 16, FEATS), F32),
            pltpu.VMEM((FEATS, 8), F32),
            dma((4,)), dma((40,)), dma((32,)), dma((16,)), dma((16,)), dma((16,)), dma((16,)), dma((16,)), dma((16,)),
        ],
        compiler_params=pltpu.CompilerParams(
            collective_id=0, has_side_effects=True, vmem_limit_bytes=48 * 1024 * 1024
        ),
    )(
        features.reshape(ROWS, FEATS),
        adj_tiles.reshape(16, SLOTS, TILE, TILE),
        cotangent.reshape(ROWS, FEATS),
        w_self,
        w_neigh,
        out_bias.reshape(1, FEATS),
        tile_rows.reshape(16, SLOTS),
        tile_cols.reshape(16, SLOTS),
        tile_count.reshape(1, 16),
        send_rows.reshape(16, HALO),
        send_count.reshape(1, 16),
        halo_weight.reshape(16, HALO),
        recv_rows.reshape(16, HALO),
    )
    return out.reshape(1, 1, ROWS, FEATS), gw, gb.reshape(FEATS)


def solution(mesh):
    placed = (
        P("grp", "dom", None, None),
        P(),
        P(),
        P(),
        P("grp", "dom", None, None, None, None),
        P("grp", "dom", None, None),
        P("grp", "dom", None, None),
        P("grp", "dom", None),
        P("grp", "dom", None, None),
        P("grp", "dom", None),
        P("grp", "dom", None, None),
        P("grp", "dom", None, None),
        P("grp", "dom", None, None),
    )
    return jax.shard_map(
        local,
        mesh=mesh,
        in_specs=placed,
        out_specs=(P("grp", "dom", None, None), P("grp", "dom"), P()),
        check_vma=False,
    )
```

time: 466 us -> 71.9 us (0.15)
  waiting for transfers between devices: 244 us -> 0 us
  blocking collectives: 72.7 us -> 0 us
  Pallas kernels: 0 us -> 57.8 us
  matrix products: 36.8 us -> 0 us
  starting transfers between devices: 34.4 us -> 0 us
  local copies, waits for them, and re-layouts: 38.5 us -> 13 us
  other arithmetic: 22.5 us -> 0 us
  between operations: 14.3 us -> 0.65 us
    psum x1 -> x0, waiting for transfers between devices: 160 us -> none  [local(): total_w, total_b = lax.psum((term_w, term_b), ('grp', 'dom'))]
    psum x1 -> x0, blocking collectives: 72.7 us -> none  [local(): total_w, total_b = lax.psum((term_w, term_b), ('grp', 'dom'))]
    ppermute x15 -> x0, waiting for transfers between devices: 72.1 us -> none  [passed_along(): return lax.ppermute(value, axis, pairs)]
    pallas_call x0 -> x1, Pallas kernels: none -> 57.8 us  [local(): pl.pallas_call(kernel, out_shape=(jax.ShapeDtypeStruct((ROWS, FEATS), BF1...]
    dot_general x38 -> x0, matrix products: 36.8 us -> none  [the longest x16 18.7 us: absorb(): jnp.einsum('sij,sjf->sif', weights, picked, preferred_element_type=jnp.fl...]
    all_to_all x2 -> x0, starting transfers between devices: 31.5 us -> none  [the longest x1 23 us: local(): lax.all_to_all(outgoing, 'dom', split_axis=0, concat_axis=0, tiled=True)]
    gather x17 -> x0, local copies, waits for them, and re-layouts: 21.7 us -> none  [the longest x1 12.1 us: local(): picked_rows = own_rows[send_index]]
    all_to_all x2 -> x0, waiting for transfers between devices: 12.3 us -> none  [the longest x1 12.3 us: local(): lax.all_to_all(outgoing, 'dom', split_axis=0, concat_axis=0, tiled=True)]
  transfers between devices with their start and end apart: 18 -> 0, of which waited for: 17 -> 0; matrix products, arithmetic and copies ran while one was open for 19% -> 0% of each run, Pallas kernels for 0% -> 0%
where the time goes in v1:
time: 71.9 us; the launch traced here: 71.4 us
  Pallas kernels  57.8 us (80%)
  local copies, waits for them, and re-layouts  13 us (18%)
    pallas_call x1, Pallas kernels, local(): pl.pallas_call(kernel, out_shape=(jax.ShapeDtypeStruct((ROWS, FEATS), BF1...  57.8 us
    unnamed x25, local copies, waits for them, and re-layouts  11.5 us

profile of v1, /device:TPU:1, one launch (start us, length us, event | category | flops | bytes accessed | tf_op | source)
XLA Modules:
  0.0 71.4 jit_solution(9914208127730608768)
XLA Ops:
  0.6 0.8 %copy.16.trows = s32[16,8]{1,0:T(8,128)S(1)} copy(s32[16,8]{0,1:T(8,128)} %bitcast.24) | data formatting | bytes 1024 | tf_op jit(solution)/shard_map/reshape | solution.py:329
  1.4 0.8 %copy.17.tcols = s32[16,8]{1,0:T(8,128)S(1)} copy(s32[16,8]{0,1:T(8,128)} %bitcast.25) | data formatting | bytes 1024 | tf_op jit(solution)/shard_map/reshape | solution.py:330
  2.1 0.0 copy-start
  2.1 2.2 %copy-done = bf16[1,1,16,8,128,128]{5,4,3,2,1,0:T(8,128)(2,1)S(1)} copy-done((bf16[1,1,16,8,128,128]{5,4,3,2,1,0:T(8,128)(2,1)S(1)}, bf16[1,1,16,8,128,128]{5,4,3,2,1,0:T(8,128)(2,1)}, u32[]{:S(2)}) %copy-start) | copy-done | bytes 4194328
  4.3 0.0 copy-start.1
  4.3 0.9 %copy-done.1 = bf16[1,1,512,128]{3,2,1,0:T(8,128)(2,1)S(1)} copy-done((bf16[1,1,512,128]{3,2,1,0:T(8,128)(2,1)S(1)}, bf16[1,1,512,128]{3,2,1,0:T(8,128)(2,1)}, u32[]{:S(2)}) %copy-start.1) | copy-done | bytes 131096
  5.2 0.0 copy-start.2
  5.2 0.9 %copy-done.2 = bf16[1,1,512,128]{3,2,1,0:T(8,128)(2,1)S(1)} copy-done((bf16[1,1,512,128]{3,2,1,0:T(8,128)(2,1)S(1)}, bf16[1,1,512,128]{3,2,1,0:T(8,128)(2,1)}, u32[]{:S(2)}) %copy-start.2) | copy-done | bytes 131096
  6.1 0.0 copy-start.3
  6.1 0.8 %copy-done.3 = bf16[128,128]{1,0:T(8,128)(2,1)S(1)} copy-done((bf16[128,128]{1,0:T(8,128)(2,1)S(1)}, bf16[128,128]{1,0:T(8,128)(2,1)}, u32[]{:S(2)}) %copy-start.3) | copy-done | bytes 32792
  6.9 0.0 copy-start.4
  6.9 0.8 %copy-done.4 = bf16[128,128]{1,0:T(8,128)(2,1)S(1)} copy-done((bf16[128,128]{1,0:T(8,128)(2,1)S(1)}, bf16[128,128]{1,0:T(8,128)(2,1)}, u32[]{:S(2)}) %copy-start.4) | copy-done | bytes 32792
  7.7 0.0 copy-start.5
  7.7 0.7 %copy-done.5 = s32[1,1,16,256]{3,2,1,0:T(8,128)S(1)} copy-done((s32[1,1,16,256]{3,2,1,0:T(8,128)S(1)}, s32[1,1,16,256]{3,2,1,0:T(8,128)}, u32[]{:S(2)}) %copy-start.5) | copy-done | bytes 16408
  8.4 0.0 copy-start.6
  8.4 0.7 %copy-done.6 = f32[1,1,16,256]{3,2,1,0:T(8,128)S(1)} copy-done((f32[1,1,16,256]{3,2,1,0:T(8,128)S(1)}, f32[1,1,16,256]{3,2,1,0:T(8,128)}, u32[]{:S(2)}) %copy-start.6) | copy-done | bytes 16408
  9.1 0.0 copy-start.7
  9.1 0.7 %copy-done.7 = s32[1,1,16,256]{3,2,1,0:T(8,128)S(1)} copy-done((s32[1,1,16,256]{3,2,1,0:T(8,128)S(1)}, s32[1,1,16,256]{3,2,1,0:T(8,128)}, u32[]{:S(2)}) %copy-start.7) | copy-done | bytes 16408
  9.8 0.0 copy-start.8
  9.8 0.7 copy-done.8
  10.5 0.0 copy-start.9
  10.5 0.7 copy-done.9
  11.1 0.0 copy-start.10
  11.1 0.7 copy-done.10
  11.8 57.8 %shard_map.148 = (bf16[512,128]{1,0:T(8,128)(2,1)S(1)}, f32[16,8]{1,0:T(8,128)S(1)}, f32[1,128]{1,0:T(1,128)S(1)}) custom-call(bf16[512,128]{1,0:T(8,128)(2,1)S(1)} %bitcast.14, bf16[16,8,128,128]{3,2,1,0:T(8,128)(2,1)S(1)} %bitcast.13, bf16[512,128]{1,0:T(8,128)(2,1)S(1)} %bitcast.15, bf16[128,128]{1,0:T(8,128)(2,1)S(1)} %copy-done.3, ...), custom_call_target="tpu_custom_call" | custom-call | tf_op jit(solution)/shard_map/pallas_call | solution.py:290
  69.6 0.7 copy.18
  70.2 0.7 copy.21
  70.9 0.5 copy.22
Async XLA Ops:
  2.1 2.2 %copy-start = (bf16[1,1,16,8,128,128]{5,4,3,2,1,0:T(8,128)(2,1)S(1)}, bf16[1,1,16,8,128,128]{5,4,3,2,1,0:T(8,128)(2,1)}, u32[]{:S(2)}) copy-start(bf16[1,1,16,8,128,128]{5,4,3,2,1,0:T(8,128)(2,1)} %param.17) | copy-start | bytes 12582916
  4.3 0.9 %copy-start.1 = (bf16[1,1,512,128]{3,2,1,0:T(8,128)(2,1)S(1)}, bf16[1,1,512,128]{3,2,1,0:T(8,128)(2,1)}, u32[]{:S(2)}) copy-start(bf16[1,1,512,128]{3,2,1,0:T(8,128)(2,1)} %param.13) | copy-start | bytes 393220
  5.2 0.9 %copy-start.2 = (bf16[1,1,512,128]{3,2,1,0:T(8,128)(2,1)S(1)}, bf16[1,1,512,128]{3,2,1,0:T(8,128)(2,1)}, u32[]{:S(2)}) copy-start(bf16[1,1,512,128]{3,2,1,0:T(8,128)(2,1)} %param.25) | copy-start | bytes 393220
  6.1 0.8 %copy-start.3 = (bf16[128,128]{1,0:T(8,128)(2,1)S(1)}, bf16[128,128]{1,0:T(8,128)(2,1)}, u32[]{:S(2)}) copy-start(bf16[128,128]{1,0:T(8,128)(2,1)} %wself.1) | copy-start | bytes 98308
  6.9 0.8 %copy-start.4 = (bf16[128,128]{1,0:T(8,128)(2,1)S(1)}, bf16[128,128]{1,0:T(8,128)(2,1)}, u32[]{:S(2)}) copy-start(bf16[128,128]{1,0:T(8,128)(2,1)} %wneigh.1) | copy-start | bytes 98308
  7.7 0.7 %copy-start.5 = (s32[1,1,16,256]{3,2,1,0:T(8,128)S(1)}, s32[1,1,16,256]{3,2,1,0:T(8,128)}, u32[]{:S(2)}) copy-start(s32[1,1,16,256]{3,2,1,0:T(8,128)} %param.21) | copy-start | bytes 49156
  8.4 0.7 %copy-start.6 = (f32[1,1,16,256]{3,2,1,0:T(8,128)S(1)}, f32[1,1,16,256]{3,2,1,0:T(8,128)}, u32[]{:S(2)}) copy-start(f32[1,1,16,256]{3,2,1,0:T(8,128)} %param.23) | copy-start | bytes 49156
  9.1 0.7 %copy-start.7 = (s32[1,1,16,256]{3,2,1,0:T(8,128)S(1)}, s32[1,1,16,256]{3,2,1,0:T(8,128)}, u32[]{:S(2)}) copy-start(s32[1,1,16,256]{3,2,1,0:T(8,128)} %param.24) | copy-start | bytes 49156
  9.8 0.7 copy-start.8
  10.5 0.7 copy-start.9
  11.1 0.7 copy-start.10

commit v2 on v1

v2 whole, which is shorter than its diff:
```python
import math

import jax
import jax.numpy as jnp
from jax import lax
from jax.experimental import pallas as pl
from jax.experimental.pallas import tpu as pltpu
from jax.sharding import PartitionSpec as P

MESH = pl.DeviceIdType.MESH
ROWS, FEATS, TILE, SLOTS, HALO = 512, 128, 128, 8, 256
HALF = ROWS // 2
NZ = 8
PAY = FEATS + 16
BF16, F32 = jnp.bfloat16, jnp.float32


def dom_hops(j):
    dy, dx = j // 4, (j // 2) % 2
    return min(dy, 4 - dy) + 2 * dx


def grp_hops(j):
    dx, dz = j // NZ, j % NZ
    return min(dz, NZ - dz) + dx


DOM_FAR = sorted(range(1, 16), key=lambda j: -dom_hops(j))
GRP_FAR = sorted(range(1, 16), key=lambda j: -grp_hops(j))


def kernel(
    feat, adj, cot_in, wself_in, wneigh_in, bias_in, trows_in, tcols_in, tcount_in, srows_in, scount_in, hweight_in,
    rrows_in,
    out, gw, gb,
    wself, wneigh, bias, trows, tcols, tcount, srows, scount, hweight, rrows,
    part, adjv, cot, stage, xcat, acc, xt, hsend, hrecv, prhs, tbuf, rec1, tb2, rec2, wmask, fx, fxt, prows, pweight,
    lsem, asend, arecv, hss, hrs, p1s, p1r, p2s, p2r, xs, xr,
):
    g, d = lax.axis_index("grp"), lax.axis_index("dom")
    xl, z = g // NZ, lax.rem(g, NZ)
    y, xh, core = d // 4, lax.rem(d // 2, 2), lax.rem(d, 2)
    up = xl * NZ + lax.rem(z + 1, NZ)
    down = xl * NZ + lax.rem(z + NZ - 1, NZ)
    side = (1 - xl) * NZ + z
    across = y * 4 + (1 - xh) * 2 + core

    def dom_to(j):
        dy, dx, dc = j // 4, lax.rem(j // 2, 2), lax.rem(j, 2)
        return lax.rem(y + dy, 4) * 4 + lax.rem(xh + dx, 2) * 2 + lax.rem(core + dc, 2)

    def grp_to(j):
        dx, dz = j // NZ, lax.rem(j, NZ)
        return lax.rem(xl + dx, 2) * NZ + lax.rem(z + dz, NZ)

    def halo_to(q):
        return lax.rem(y + q // 2, 4) * 4 + xh * 2 + lax.rem(core + lax.rem(q, 2), 2)

    def halo_from(slot):
        q = lax.rem(slot, 8)
        return lax.rem(y + 4 - q // 2, 4) * 4 + lax.rem(xh + slot // 8, 2) * 2 + lax.rem(core + lax.rem(q, 2), 2)

    def load(n, source, target):
        copy = pltpu.make_async_copy(source, target, lsem.at[n])
        copy.start()
        return copy

    load_x = load(0, feat, part.at[0])
    load_h = [load(1, srows_in, srows), load(2, scount_in, scount), load(3, hweight_in, hweight)]
    load_t = [load(4, trows_in, trows), load(5, tcols_in, tcols), load(6, tcount_in, tcount)]
    load_a = load(7, adj, adjv)
    load_r = load(8, rrows_in, rrows)
    load_w = [load(9, wself_in, wself), load(10, wneigh_in, wneigh), load(11, bias_in, bias), load(12, cot_in, cot)]

    barrier = pltpu.get_barrier_semaphore()
    for q in (4, 5, 2, 3, 6, 7, 1):
        pl.semaphore_signal(barrier, inc=1, device_id=(g, halo_to(q)), device_id_type=MESH)
    pl.semaphore_signal(barrier, inc=1, device_id=(g, across), device_id_type=MESH)
    for to in (up, down, side):
        pl.semaphore_signal(barrier, inc=1, device_id=(to, d), device_id_type=MESH)

    for copy in load_h:
        copy.wait()
    lane = lax.broadcasted_iota(jnp.int32, (1, HALO), 1)
    for j in range(16):
        wmask[j:j + 1, :] = jnp.where(lane < scount[0, j], hweight[j:j + 1, :], 0.0)
    load_x.wait()
    xt[...] = part[0].T
    acc[...] = jnp.zeros_like(acc)
    xcat[:, FEATS:] = jnp.ones((SLOTS * TILE, FEATS), BF16)
    node = lax.broadcasted_iota(jnp.int32, (ROWS, HALO), 0)

    def build_halo(block, table, weights, to, target):
        pick = jnp.where(node == table[pl.ds(to, 1), :], 1.0, 0.0).astype(BF16)
        weight = weights[pl.ds(to, 1), :]
        rows = jnp.dot(block[...], pick, preferred_element_type=F32)
        target[0:FEATS, :] = (rows * weight).astype(BF16)
        target[FEATS:PAY, :] = jnp.broadcast_to(weight, (PAY - FEATS, HALO)).astype(BF16)

    def halo_copy(slot):
        return pltpu.make_async_remote_copy(
            src_ref=hsend.at[slot], dst_ref=hrecv.at[slot], send_sem=hss.at[slot], recv_sem=hrs.at[slot],
            device_id=(g, halo_to(lax.rem(slot, 8))), device_id_type=MESH,
        )

    def across_copy(n, source, target):
        return pltpu.make_async_remote_copy(
            src_ref=source, dst_ref=target, send_sem=xs.at[n], recv_sem=xr.at[n],
            device_id=(g, across), device_id_type=MESH,
        )

    sent = []

    def send(slot_from, slot_to, h, to):
        n = len(sent)
        copy = pltpu.make_async_remote_copy(
            src_ref=part.at[slot_from, pl.ds(h * HALF, HALF), :],
            dst_ref=part.at[slot_to, pl.ds(h * HALF, HALF), :],
            send_sem=asend.at[n], recv_sem=arecv.at[2 * slot_to + h],
            device_id=(to, d), device_id_type=MESH,
        )
        copy.start()
        sent.append(copy)

    def landed(slot, h):
        pltpu.make_async_remote_copy(
            src_ref=part.at[slot, pl.ds(h * HALF, HALF), :],
            dst_ref=part.at[slot, pl.ds(h * HALF, HALF), :],
            send_sem=asend.at[0], recv_sem=arecv.at[2 * slot + h],
            device_id=(up, d), device_id_type=MESH,
        ).wait_recv()

    def absorb(slot, source):
        stage[...] = part[slot].reshape(4, TILE, FEATS)
        for s in range(SLOTS):
            xcat[s * TILE:(s + 1) * TILE, 0:FEATS] = stage[tcols[s, source]]
        limit = jnp.full((16, TILE), tcount[0, source], jnp.int32)
        for r in range(4):
            kept = []
            for s in range(SLOTS):
                target = jnp.full((16, TILE), trows[s, source], jnp.int32)
                on = jnp.where((target == r) & (limit > s), 1.0, 0.0).astype(BF16)
                kept.append(adjv[source, s] * jnp.concatenate([on] * (TILE // 16), axis=0))
            acc[r * TILE:(r + 1) * TILE, :] += jnp.dot(
                jnp.concatenate(kept, axis=1), xcat[...], preferred_element_type=F32
            )

    def absorb_step(first, count, dist):
        def body(k, _):
            source = lax.rem(xl + k // 2, 2) * NZ + lax.rem(z + NZ + dist * (2 * lax.rem(k, 2) - 1), NZ)
            absorb(first + k, source)
            return 0
        lax.fori_loop(0, count, body, 0)

    def take_halo(slot):
        source = halo_from(slot)
        prhs[0:FEATS, :] = hrecv[slot, 0:FEATS, :]
        weights = hrecv[slot, FEATS:PAY, :]
        for i in range(FEATS // 16):
            prhs[FEATS + 16 * i:FEATS + 16 * (i + 1), :] = weights
        hits = jnp.where(node == rrows[pl.ds(source, 1), :], 1.0, 0.0).astype(BF16)
        acc[...] += lax.dot_general(hits, prhs[...], (((1,), (1,)), ((), ())), preferred_element_type=F32)

    def take_halos(lo, hi):
        def body(slot, _):
            halo_copy(slot).wait_recv()
            take_halo(slot)
            return 0
        lax.fori_loop(lo, hi, body, 0)

    pl.semaphore_wait(barrier, 11)

    send(0, 1, 1, side)
    send(0, 2, 0, up)
    send(0, 3, 0, down)
    crossing = [
        across_copy(0, srows, prows), across_copy(1, wmask, pweight), across_copy(2, part.at[0], fx),
    ]
    for copy in crossing:
        copy.start()
    send(0, 2, 1, up)
    send(0, 3, 1, down)
    send(0, 1, 0, side)

    @pl.loop(1, 8)
    def _(q):
        build_halo(xt, srows, wmask, halo_to(q), hsend.at[q])
        halo_copy(q).start()

    landed(1, 1)
    send(1, 4, 1, up)
    send(1, 5, 1, down)
    load_a.wait()
    load_r.wait()
    for copy in load_t:
        copy.wait()
    for dist in (1, 2):
        a = 4 * dist - 2
        landed(a, 0)
        send(a, a + 4, 0, up)
        send(a, a + 2, 0, side)
        landed(a + 1, 0)
        send(a + 1, a + 5, 0, down)
        send(a + 1, a + 3, 0, side)
        landed(a, 1)
        send(a, a + 4, 1, up)
        landed(a + 1, 1)
        send(a + 1, a + 5, 1, down)
        landed(a + 2, 1)
        send(a + 2, a + 6, 1, up)
        landed(a + 3, 1)
        send(a + 3, a + 7, 1, down)
        if dist == 1:
            for copy in crossing:
                copy.wait_recv()
            fxt[...] = fx[...].T

            @pl.loop(1, 8)
            def _(q):
                build_halo(fxt, prows, pweight, halo_to(q), hsend.at[8 + q])
                halo_copy(8 + q).start()

            build_halo(fxt, prows, pweight, halo_to(0), hrecv.at[8])
            landed(1, 0)
            absorb(0, g)
            absorb(1, side)
        else:
            landed(4, 0)
            landed(5, 0)
            absorb_step(2, 4, 1)
            take_halo(8)
    landed(10, 0)
    send(10, 14, 0, up)
    send(10, 12, 0, side)
    landed(11, 0)
    send(11, 13, 0, side)
    landed(10, 1)
    landed(11, 1)
    send(11, 14, 1, down)
    landed(12, 1)
    send(12, 15, 1, up)
    landed(13, 1)
    landed(8, 0)
    landed(9, 0)
    absorb_step(6, 4, 2)
    take_halos(1, 5)
    landed(14, 0)
    send(14, 15, 0, side)
    landed(12, 0)
    landed(13, 0)
    absorb_step(10, 4, 3)
    take_halos(5, 8)
    landed(14, 1)
    absorb_step(14, 1, 4)
    take_halos(9, 16)
    landed(15, 1)
    landed(15, 0)
    absorb(15, lax.rem(xl + 1, 2) * NZ + lax.rem(z + 4, NZ))

    for copy in load_w:
        copy.wait()
    wcat = jnp.concatenate([wself[...], wneigh[...]], axis=0)
    bias_row = bias[...]
    total_b = jnp.zeros((1, FEATS), F32)
    total_w = jnp.zeros((FEATS, 2 * FEATS), F32)
    for r in range(4):
        rs = pl.ds(r * TILE, TILE)
        agg = (acc[rs, 0:FEATS] * lax.rsqrt(1.0 + acc[rs, FEATS:])).astype(BF16)
        cat = jnp.concatenate([part[0, rs, :], agg], axis=1)
        pre = jnp.dot(cat, wcat, preferred_element_type=F32) + bias_row
        sig = jax.nn.sigmoid(pre)
        out[rs, :] = (pre * sig).astype(BF16)
        slope = (cot[rs, :].astype(F32) * sig * (1.0 + pre * (1.0 - sig))).astype(BF16)
        total_b += jnp.sum(slope.astype(F32), axis=0, keepdims=True)
        total_w += lax.dot_general(slope, cat, (((0,), (0,)), ((), ())), preferred_element_type=F32)
    tbuf[:, 0:8, :] = total_w[:, 0:FEATS].reshape(16, 8, FEATS)
    tbuf[:, 8:16, :] = total_w[:, FEATS:].reshape(16, 8, FEATS)
    tbuf[:, 16:24, :] = jnp.broadcast_to(total_b[None], (16, 8, FEATS))

    def first_copy(j):
        return pltpu.make_async_remote_copy(
            src_ref=tbuf.at[dom_to(j), pl.ds(0, 17), :], dst_ref=rec1.at[j, pl.ds(0, 17), :],
            send_sem=p1s.at[j], recv_sem=p1r.at[j],
            device_id=(g, dom_to(j)), device_id_type=MESH,
        )

    def second_copy(j):
        return pltpu.make_async_remote_copy(
            src_ref=tb2.at[grp_to(j), pl.ds(0, 2), :], dst_ref=rec2.at[j, pl.ds(0, 2), :],
            send_sem=p2s.at[j], recv_sem=p2r.at[j],
            device_id=(grp_to(j), d), device_id_type=MESH,
        )

    for j in DOM_FAR:
        first_copy(j).start()

    for copy in sent + crossing:
        copy.wait_send()

    @pl.loop(1, 8)
    def _(q):
        halo_copy(q).wait_send()
        halo_copy(8 + q).wait_send()

    red_w, red_b = tbuf[d, 0:16, :], tbuf[d, 16:17, :]
    for j in DOM_FAR[::-1]:
        first_copy(j).wait_recv()
        red_w += rec1[j, 0:16, :]
        red_b += rec1[j, 16:17, :]

    row8 = lax.broadcasted_iota(jnp.int32, (8, FEATS), 0)
    block16 = lax.broadcasted_iota(jnp.int32, (8, FEATS), 1) // 16
    for half in range(2):
        tile = red_w[8 * half:8 * half + 8]
        turned = jnp.zeros((8, FEATS), F32)
        for k in range(8):
            moved = tile if k == 0 else pltpu.roll(tile, 16 * k, 1)
            moved = jnp.where(row8 == block16, moved, 0.0)
            turned += moved if k == 0 else pltpu.roll(moved, 8 - k, 0)
        for p in range(8):
            tb2[8 * half + p, 0:1, :] = turned[p:p + 1]
            tb2[8 * half + p, 1:2, :] = red_b
    for j in GRP_FAR:
        second_copy(j).start()
    fin = tb2[g, 0:2, :]
    for j in GRP_FAR[::-1]:
        second_copy(j).wait_recv()
        fin += rec2[j, 0:2, :]
    fin *= 1.0 / math.sqrt(ROWS * 256)
    for c in range(8):
        gw[c:c + 1, :] = fin[0:1, 16 * c:16 * c + 16]
    gb[...] = fin[1:2]

    @pl.loop(1, 16)
    def _(j):
        first_copy(j).wait_send()
        second_copy(j).wait_send()


def local(
    features, w_self, w_neigh, out_bias, adj_tiles, tile_rows, tile_cols, tile_count, send_rows,
    send_count, halo_weight, recv_rows, cotangent,
):
    hbm = pl.BlockSpec(memory_space=pltpu.HBM)
    vmem = pl.BlockSpec(memory_space=pltpu.VMEM)
    dma = pltpu.SemaphoreType.DMA
    out, gw, gb = pl.pallas_call(
        kernel,
        out_shape=(
            jax.ShapeDtypeStruct((ROWS, FEATS), BF16),
            jax.ShapeDtypeStruct((8, 16), F32),
            jax.ShapeDtypeStruct((1, FEATS), F32),
        ),
        in_specs=[hbm] * 13,
        out_specs=(vmem, vmem, vmem),
        scratch_shapes=[
            pltpu.VMEM((FEATS, FEATS), BF16),
            pltpu.VMEM((FEATS, FEATS), BF16),
            pltpu.VMEM((1, FEATS), F32),
            pltpu.SMEM((SLOTS, 16), jnp.int32),
            pltpu.SMEM((SLOTS, 16), jnp.int32),
            pltpu.SMEM((1, 16), jnp.int32),
            pltpu.VMEM((16, HALO), jnp.int32),
            pltpu.SMEM((1, 16), jnp.int32),
            pltpu.VMEM((16, HALO), F32),
            pltpu.VMEM((16, HALO), jnp.int32),
            pltpu.VMEM((16, ROWS, FEATS), BF16),
            pltpu.VMEM((16, SLOTS, TILE, TILE), BF16),
            pltpu.VMEM((ROWS, FEATS), BF16),
            pltpu.VMEM((4, TILE, FEATS), BF16),
            pltpu.VMEM((SLOTS * TILE, 2 * FEATS), BF16),
            pltpu.VMEM((ROWS, 2 * FEATS), F32),
            pltpu.VMEM((FEATS, ROWS), BF16),
            pltpu.VMEM((16, PAY, HALO), BF16),
            pltpu.VMEM((16, PAY, HALO), BF16),
            pltpu.VMEM((2 * FEATS, HALO), BF16),
            pltpu.VMEM((16, 24, FEATS), F32),
            pltpu.VMEM((16, 24, FEATS), F32),
            pltpu.VMEM((16, 8, FEATS), F32),
            pltpu.VMEM((16, 8, FEATS), F32),
            pltpu.VMEM((16, HALO), F32),
            pltpu.VMEM((ROWS, FEATS), BF16),
            pltpu.VMEM((FEATS, ROWS), BF16),
            pltpu.VMEM((16, HALO), jnp.int32),
            pltpu.VMEM((16, HALO), F32),
            dma((16,)), dma((40,)), dma((32,)), dma((16,)), dma((16,)), dma((16,)), dma((16,)), dma((16,)), dma((16,)),
            dma((3,)), dma((3,)),
        ],
        compiler_params=pltpu.CompilerParams(
            collective_id=0, has_side_effects=True, vmem_limit_bytes=40 * 1024 * 1024
        ),
    )(*(pltpu.with_memory_space_constraint(value, pltpu.HBM) for value in (
        features.reshape(ROWS, FEATS),
        adj_tiles.reshape(16, SLOTS, TILE, TILE),
        cotangent.reshape(ROWS, FEATS),
        w_self,
        w_neigh,
        out_bias.reshape(1, FEATS),
        tile_rows.reshape(16, SLOTS).T,
        tile_cols.reshape(16, SLOTS).T,
        tile_count.reshape(1, 16),
        send_rows.reshape(16, HALO),
        send_count.reshape(1, 16),
        halo_weight.reshape(16, HALO),
        recv_rows.reshape(16, HALO),
    )))
    return out.reshape(1, 1, ROWS, FEATS), gw.T, gb.reshape(FEATS)


def solution(mesh):
    placed = (
        P("grp", "dom", None, None),
        P(),
        P(),
        P(),
        P("grp", "dom", None, None, None, None),
        P("grp", "dom", None, None),
        P("grp", "dom", None, None),
        P("grp", "dom", None),
        P("grp", "dom", None, None),
        P("grp", "dom", None),
        P("grp", "dom", None, None),
        P("grp", "dom", None, None),
        P("grp", "dom", None, None),
    )
    return jax.shard_map(
        local,
        mesh=mesh,
        in_specs=placed,
        out_specs=(P("grp", "dom", None, None), P("grp", "dom"), P()),
        check_vma=False,
    )
```

time: 71.9 us -> 49.1 us (0.68)
  local copies, waits for them, and re-layouts: 13 us -> 1.76 us
  Pallas kernels: 57.8 us -> 46.7 us
    pallas_call x1, Pallas kernels: 57.8 us -> 46.7 us  [local(): pl.pallas_call(kernel, out_shape=(jax.ShapeDtypeStruct((ROWS, FEATS), BF1...]
    unnamed x25 -> x3, local copies, waits for them, and re-layouts: 11.5 us -> 1.76 us
    reshape x2 -> x0, local copies, waits for them, and re-layouts: 1.52 us -> none  [the longest x1 0.76 us: local(): tile_rows.reshape(16, SLOTS)]
where the time goes in v2:
time: 49.1 us
  Pallas kernels  46.7 us (95%)
  local copies, waits for them, and re-layouts  1.76 us (4%)
  between operations  0.64 us (1%)
    pallas_call x1, Pallas kernels, local(): pl.pallas_call(kernel, out_shape=(jax.ShapeDtypeStruct((ROWS, FEATS), BF1...  46.7 us
    unnamed x3, local copies, waits for them, and re-layouts  1.76 us

profile of v2, /device:TPU:1, one launch (start us, length us, event | category | flops | bytes accessed | tf_op | source)
XLA Modules:
  0.0 49.1 jit_solution(2684831214838143036)
XLA Ops:
  0.6 46.7 %shard_map.148 = (bf16[512,128]{1,0:T(8,128)(2,1)S(1)}, f32[8,16]{1,0:T(8,128)S(1)}, f32[1,128]{1,0:T(1,128)S(1)}) custom-call(bf16[512,128]{1,0:T(8,128)(2,1)} %bitcast.22, bf16[16,8,128,128]{3,2,1,0:T(8,128)(2,1)} %bitcast.21, bf16[512,128]{1,0:T(8,128)(2,1)} %bitcast.23, bf16[128,128]{1,0:T(8,128)(2,1)} %wself_in.1, bf16[128,128]{1,0:T(8,128)(2,1)} %wneigh_in.1, ...), custom_call_target="tpu_custom_call" | custom-call | tf_op jit(solution)/shard_map/pallas_call | solution.py:347
  47.3 0.7 %copy.19 = bf16[1,1,512,128]{3,2,1,0:T(8,128)(2,1)} copy(bf16[1,1,512,128]{3,2,1,0:T(8,128)(2,1)S(1)} %bitcast.18) | data formatting | bytes 262144
  48.0 0.6 %copy.20 = f32[16,8]{0,1:T(8,128)} copy(f32[16,8]{0,1:T(8,128)S(1)} %bitcast.19) | data formatting | bytes 1024
  48.5 0.5 %copy.21 = f32[128]{0:T(128)} copy(f32[128]{0:T(128)S(1)} %bitcast.20) | data formatting | bytes 1024

commit v3 on v2

--- a/solution.py
+++ b/solution.py
@@ -27,6 +27,7 @@
 
 DOM_FAR = sorted(range(1, 16), key=lambda j: -dom_hops(j))
 GRP_FAR = sorted(range(1, 16), key=lambda j: -grp_hops(j))
+PIECES = ((0, HALF), (HALF, HALF), (HALF, HALF // 2), (HALF + HALF // 2, HALF // 2))
 
 
 def kernel(
@@ -34,7 +35,7 @@
     rrows_in,
     out, gw, gb,
     wself, wneigh, bias, trows, tcols, tcount, srows, scount, hweight, rrows,
-    part, adjv, cot, stage, xcat, acc, xt, hsend, hrecv, prhs, tbuf, rec1, tb2, rec2, wmask, fx, fxt, prows, pweight,
+    part, adjv, cot, stage, acc, xt, hsend, hrecv, prhs, tbuf, rec1, tb2, rec2, wmask, fx, fxt, prows, pweight, table, plan, segment, degree,
     lsem, asend, arecv, hss, hrs, p1s, p1r, p2s, p2r, xs, xr,
 ):
     g, d = lax.axis_index("grp"), lax.axis_index("dom")
@@ -87,7 +88,8 @@
     load_x.wait()
     xt[...] = part[0].T
     acc[...] = jnp.zeros_like(acc)
-    xcat[:, FEATS:] = jnp.ones((SLOTS * TILE, FEATS), BF16)
+    segment[8] = jnp.zeros((TILE, FEATS), F32)
+    degree[...] = jnp.zeros((TILE, FEATS), F32)
     node = lax.broadcasted_iota(jnp.int32, (ROWS, HALO), 0)
 
     def build_halo(block, table, weights, to, target):
@@ -111,46 +113,85 @@
 
     sent = []
 
-    def send(slot_from, slot_to, h, to):
+    def send(slot_from, slot_to, piece, to):
         n = len(sent)
+        rows = pl.ds(*PIECES[piece])
         copy = pltpu.make_async_remote_copy(
-            src_ref=part.at[slot_from, pl.ds(h * HALF, HALF), :],
-            dst_ref=part.at[slot_to, pl.ds(h * HALF, HALF), :],
-            send_sem=asend.at[n], recv_sem=arecv.at[2 * slot_to + h],
+            src_ref=part.at[slot_from, rows, :], dst_ref=part.at[slot_to, rows, :],
+            send_sem=asend.at[n], recv_sem=arecv.at[4 * slot_to + piece],
             device_id=(to, d), device_id_type=MESH,
         )
         copy.start()
         sent.append(copy)
 
-    def landed(slot, h):
+    def landed(slot, piece):
+        rows = pl.ds(*PIECES[piece])
         pltpu.make_async_remote_copy(
-            src_ref=part.at[slot, pl.ds(h * HALF, HALF), :],
-            dst_ref=part.at[slot, pl.ds(h * HALF, HALF), :],
-            send_sem=asend.at[0], recv_sem=arecv.at[2 * slot + h],
+            src_ref=part.at[slot, rows, :], dst_ref=part.at[slot, rows, :],
+            send_sem=asend.at[0], recv_sem=arecv.at[4 * slot + piece],
             device_id=(up, d), device_id_type=MESH,
         ).wait_recv()
 
+    def sort_slots():
+        count = tcount[...]
+        keys = [jnp.where(count > s, trows[s:s + 1, :], 4) for s in range(SLOTS)]
+        one = jnp.ones((1, 16), jnp.int32)
+        none = jnp.zeros((1, 16), jnp.int32)
+        rank = []
+        for s in range(SLOTS):
+            total = none
+            for t in range(SLOTS):
+                if t != s:
+                    ahead = keys[t] <= keys[s] if t < s else keys[t] < keys[s]
+                    total += jnp.where(ahead, one, none)
+            rank.append(total)
+        for i in range(SLOTS):
+            at, column, key = none, none, none
+            for s in range(SLOTS):
+                here = rank[s] == i
+                at += jnp.where(here, s * one, none)
+                column += jnp.where(here, tcols[s:s + 1, :], none)
+                key += jnp.where(here, keys[s], none)
+            table[i:i + 1, :] = at
+            table[8 + i:9 + i, :] = column
+            table[16 + i:17 + i, :] = key
+        for r in range(4):
+            upto, equal = none, none
+            for s in range(SLOTS):
+                upto += jnp.where(keys[s] <= r, one, none)
+                equal += jnp.where(keys[s] == r, one, none)
+            table[24 + r:25 + r, :] = jnp.where(equal > 0, upto - 1, 8)
+        copy = pltpu.make_async_copy(table, plan, lsem.at[13])
+        copy.start()
+        return copy
+
+    lane16 = lax.broadcasted_iota(jnp.int32, (16, FEATS), 1)
+
     def absorb(slot, source):
         stage[...] = part[slot].reshape(4, TILE, FEATS)
-        for s in range(SLOTS):
-            xcat[s * TILE:(s + 1) * TILE, 0:FEATS] = stage[tcols[s, source]]
-        limit = jnp.full((16, TILE), tcount[0, source], jnp.int32)
+        running, before, tiles, marks = None, None, [], []
+        for i in range(SLOTS):
+            tile = adjv[source, plan[i, source]]
+            product = jnp.dot(tile, stage[plan[8 + i, source]], preferred_element_type=F32)
+            key = jnp.full((16, FEATS), plan[16 + i, source], jnp.int32)
+            tiles.append(tile)
+            marks += [jnp.where(lane16 == key, 1.0, 0.0).astype(BF16)] * (TILE // 16)
+            if i:
+                same = jnp.concatenate([jnp.where(key == before, 1, 0)] * (TILE // 16), axis=0) > 0
+                product += jnp.where(same, running, 0.0)
+            running, before = product, key
+            segment[i] = running
+        degree[...] += jnp.dot(
+            jnp.concatenate(tiles, axis=1), jnp.concatenate(marks, axis=0), preferred_element_type=F32
+        )
         for r in range(4):
-            kept = []
-            for s in range(SLOTS):
-                target = jnp.full((16, TILE), trows[s, source], jnp.int32)
-                on = jnp.where((target == r) & (limit > s), 1.0, 0.0).astype(BF16)
-                kept.append(adjv[source, s] * jnp.concatenate([on] * (TILE // 16), axis=0))
-            acc[r * TILE:(r + 1) * TILE, :] += jnp.dot(
-                jnp.concatenate(kept, axis=1), xcat[...], preferred_element_type=F32
-            )
-
-    def absorb_step(first, count, dist):
+            acc[r * TILE:(r + 1) * TILE, 0:FEATS] += segment[plan[24 + r, source]]
+
+    def absorb_pair(first, dist, column):
         def body(k, _):
-            source = lax.rem(xl + k // 2, 2) * NZ + lax.rem(z + NZ + dist * (2 * lax.rem(k, 2) - 1), NZ)
-            absorb(first + k, source)
+            absorb(first + k, column * NZ + lax.rem(z + NZ + dist * (2 * k - 1), NZ))
             return 0
-        lax.fori_loop(0, count, body, 0)
+        lax.fori_loop(0, 2, body, 0)
 
     def take_halo(slot):
         source = halo_from(slot)
@@ -187,75 +228,93 @@
         build_halo(xt, srows, wmask, halo_to(q), hsend.at[q])
         halo_copy(q).start()
 
+    for copy in load_t:
+        copy.wait()
+    planned = sort_slots()
+    other = 1 - xl
+    landed(2, 0)
+    send(2, 6, 0, up)
+    send(2, 4, 0, side)
+    landed(3, 0)
+    send(3, 7, 0, down)
+    send(3, 5, 0, side)
     landed(1, 1)
     send(1, 4, 1, up)
     send(1, 5, 1, down)
     load_a.wait()
     load_r.wait()
-    for copy in load_t:
-        copy.wait()
-    for dist in (1, 2):
-        a = 4 * dist - 2
-        landed(a, 0)
-        send(a, a + 4, 0, up)
-        send(a, a + 2, 0, side)
-        landed(a + 1, 0)
-        send(a + 1, a + 5, 0, down)
-        send(a + 1, a + 3, 0, side)
-        landed(a, 1)
-        send(a, a + 4, 1, up)
-        landed(a + 1, 1)
-        send(a + 1, a + 5, 1, down)
-        landed(a + 2, 1)
-        send(a + 2, a + 6, 1, up)
-        landed(a + 3, 1)
-        send(a + 3, a + 7, 1, down)
-        if dist == 1:
-            for copy in crossing:
-                copy.wait_recv()
-            fxt[...] = fx[...].T
-
-            @pl.loop(1, 8)
-            def _(q):
-                build_halo(fxt, prows, pweight, halo_to(q), hsend.at[8 + q])
-                halo_copy(8 + q).start()
-
-            build_halo(fxt, prows, pweight, halo_to(0), hrecv.at[8])
-            landed(1, 0)
-            absorb(0, g)
-            absorb(1, side)
-        else:
-            landed(4, 0)
-            landed(5, 0)
-            absorb_step(2, 4, 1)
-            take_halo(8)
+    planned.wait()
+    absorb(0, g)
+    landed(2, 1)
+    send(2, 6, 1, up)
+    landed(3, 1)
+    send(3, 7, 1, down)
+    for copy in crossing:
+        copy.wait_recv()
+    fxt[...] = fx[...].T
+
+    @pl.loop(1, 8)
+    def _(q):
+        build_halo(fxt, prows, pweight, halo_to(q), hsend.at[8 + q])
+        halo_copy(8 + q).start()
+
+    landed(6, 0)
+    send(6, 10, 0, up)
+    send(6, 8, 0, side)
+    landed(7, 0)
+    send(7, 11, 0, down)
+    send(7, 9, 0, side)
+    absorb_pair(2, 1, xl)
+    landed(4, 1)
+    send(4, 8, 1, up)
+    landed(5, 1)
+    send(5, 9, 1, down)
+    landed(1, 0)
+    absorb(1, side)
+    build_halo(fxt, prows, pweight, halo_to(0), hrecv.at[8])
+    take_halo(8)
+    landed(6, 1)
+    send(6, 10, 1, up)
+    landed(7, 1)
+    send(7, 11, 1, down)
+    absorb_pair(6, 2, xl)
     landed(10, 0)
     send(10, 14, 0, up)
     send(10, 12, 0, side)
     landed(11, 0)
     send(11, 13, 0, side)
+    landed(4, 0)
+    landed(5, 0)
+    absorb_pair(4, 1, other)
+    landed(8, 1)
+    send(8, 12, 1, up)
+    landed(9, 1)
+    send(9, 13, 1, down)
+    take_halos(1, 5)
     landed(10, 1)
     landed(11, 1)
     send(11, 14, 1, down)
-    landed(12, 1)
-    send(12, 15, 1, up)
-    landed(13, 1)
+    absorb_pair(10, 3, xl)
+    landed(14, 0)
+    send(14, 15, 0, side)
     landed(8, 0)
     landed(9, 0)
-    absorb_step(6, 4, 2)
-    take_halos(1, 5)
-    landed(14, 0)
-    send(14, 15, 0, side)
+    absorb_pair(8, 2, other)
+    landed(12, 1)
+    send(12, 15, 2, up)
+    landed(13, 1)
+    send(13, 15, 3, down)
+    landed(14, 1)
+    absorb(14, xl * NZ + lax.rem(z + 4, NZ))
+    take_halos(5, 8)
+    take_halos(9, 16)
     landed(12, 0)
     landed(13, 0)
-    absorb_step(10, 4, 3)
-    take_halos(5, 8)
-    landed(14, 1)
-    absorb_step(14, 1, 4)
-    take_halos(9, 16)
-    landed(15, 1)
+    absorb_pair(12, 3, other)
+    landed(15, 2)
+    landed(15, 3)
     landed(15, 0)
-    absorb(15, lax.rem(xl + 1, 2) * NZ + lax.rem(z + 4, NZ))
+    absorb(15, other * NZ + lax.rem(z + 4, NZ))
 
     for copy in load_w:
         copy.wait()
@@ -265,7 +324,8 @@
     total_w = jnp.zeros((FEATS, 2 * FEATS), F32)
     for r in range(4):
         rs = pl.ds(r * TILE, TILE)
-        agg = (acc[rs, 0:FEATS] * lax.rsqrt(1.0 + acc[rs, FEATS:])).astype(BF16)
+        total = 1.0 + acc[rs, FEATS:] + jnp.broadcast_to(degree[:, r:r + 1], (TILE, FEATS))
+        agg = (acc[rs, 0:FEATS] * lax.rsqrt(total)).astype(BF16)
         cat = jnp.concatenate([part[0, rs, :], agg], axis=1)
         pre = jnp.dot(cat, wcat, preferred_element_type=F32) + bias_row
         sig = jax.nn.sigmoid(pre)
@@ -357,9 +417,9 @@
             pltpu.VMEM((FEATS, FEATS), BF16),
             pltpu.VMEM((FEATS, FEATS), BF16),
             pltpu.VMEM((1, FEATS), F32),
-            pltpu.SMEM((SLOTS, 16), jnp.int32),
-            pltpu.SMEM((SLOTS, 16), jnp.int32),
-            pltpu.SMEM((1, 16), jnp.int32),
+            pltpu.VMEM((SLOTS, 16), jnp.int32),
+            pltpu.VMEM((SLOTS, 16), jnp.int32),
+            pltpu.VMEM((1, 16), jnp.int32),
             pltpu.VMEM((16, HALO), jnp.int32),
             pltpu.SMEM((1, 16), jnp.int32),
             pltpu.VMEM((16, HALO), F32),
@@ -368,7 +428,6 @@
             pltpu.VMEM((16, SLOTS, TILE, TILE), BF16),
             pltpu.VMEM((ROWS, FEATS), BF16),
             pltpu.VMEM((4, TILE, FEATS), BF16),
-            pltpu.VMEM((SLOTS * TILE, 2 * FEATS), BF16),
             pltpu.VMEM((ROWS, 2 * FEATS), F32),
             pltpu.VMEM((FEATS, ROWS), BF16),
             pltpu.VMEM((16, PAY, HALO), BF16),
@@ -383,7 +442,11 @@
             pltpu.VMEM((FEATS, ROWS), BF16),
             pltpu.VMEM((16, HALO), jnp.int32),
             pltpu.VMEM((16, HALO), F32),
-            dma((16,)), dma((40,)), dma((32,)), dma((16,)), dma((16,)), dma((16,)), dma((16,)), dma((16,)), dma((16,)),
+            pltpu.VMEM((32, 16), jnp.int32),
+            pltpu.SMEM((32, 16), jnp.int32),
+            pltpu.VMEM((9, TILE, FEATS), F32),
+            pltpu.VMEM((TILE, FEATS), F32),
+            dma((16,)), dma((40,)), dma((64,)), dma((16,)), dma((16,)), dma((16,)), dma((16,)), dma((16,)), dma((16,)),
             dma((3,)), dma((3,)),
         ],
         compiler_params=pltpu.CompilerParams(

time: 49.1 us -> 47.1 us (0.959)
  Pallas kernels: 46.7 us -> 44.6 us
    pallas_call x1, Pallas kernels: 46.7 us -> 44.6 us  [local(): pl.pallas_call(kernel, out_shape=(jax.ShapeDtypeStruct((ROWS, FEATS), BF1...]
where the time goes in v3:
time: 47.1 us; the launch traced here: 47 us
  Pallas kernels  44.6 us (95%)
  local copies, waits for them, and re-layouts  1.76 us (4%)
  between operations  0.64 us (1%)
    pallas_call x1, Pallas kernels, local(): pl.pallas_call(kernel, out_shape=(jax.ShapeDtypeStruct((ROWS, FEATS), BF1...  44.6 us
    unnamed x3, local copies, waits for them, and re-layouts  1.76 us

profile of v3, /device:TPU:1, one launch (start us, length us, event | category | flops | bytes accessed | tf_op | source)
XLA Modules:
  0.0 47.0 jit_solution(7396718903440923394)
XLA Ops:
  0.6 44.6 %shard_map.148 = (bf16[512,128]{1,0:T(8,128)(2,1)S(1)}, f32[8,16]{1,0:T(8,128)S(1)}, f32[1,128]{1,0:T(1,128)S(1)}) custom-call(bf16[512,128]{1,0:T(8,128)(2,1)} %bitcast.22, bf16[16,8,128,128]{3,2,1,0:T(8,128)(2,1)} %bitcast.21, bf16[512,128]{1,0:T(8,128)(2,1)} %bitcast.23, bf16[128,128]{1,0:T(8,128)(2,1)} %wself_in.1, bf16[128,128]{1,0:T(8,128)(2,1)} %wneigh_in.1, ...), custom_call_target="tpu_custom_call" | custom-call | tf_op jit(solution)/shard_map/pallas_call | solution.py:407
  45.3 0.7 %copy.19 = bf16[1,1,512,128]{3,2,1,0:T(8,128)(2,1)} copy(bf16[1,1,512,128]{3,2,1,0:T(8,128)(2,1)S(1)} %bitcast.18) | data formatting | bytes 262144
  45.9 0.6 %copy.20 = f32[16,8]{0,1:T(8,128)} copy(f32[16,8]{0,1:T(8,128)S(1)} %bitcast.19) | data formatting | bytes 1024
  46.5 0.5 %copy.21 = f32[128]{0:T(128)} copy(f32[128]{0:T(128)S(1)} %bitcast.20) | data formatting | bytes 1024

commit v4 on v3

--- a/solution.py
+++ b/solution.py
@@ -35,7 +35,7 @@
     rrows_in,
     out, gw, gb,
     wself, wneigh, bias, trows, tcols, tcount, srows, scount, hweight, rrows,
-    part, adjv, cot, stage, acc, xt, hsend, hrecv, prhs, tbuf, rec1, tb2, rec2, wmask, fx, fxt, prows, pweight, table, plan, segment, degree,
+    part, adjv, cot, stage, acc, xt, hsend, hrecv, tbuf, rec1, tb2, rec2, wmask, fx, fxt, prows, pweight, table, plan, segment, degree,
     lsem, asend, arecv, hss, hrs, p1s, p1r, p2s, p2r, xs, xr,
 ):
     g, d = lax.axis_index("grp"), lax.axis_index("dom")
@@ -193,21 +193,15 @@
             return 0
         lax.fori_loop(0, 2, body, 0)
 
-    def take_halo(slot):
-        source = halo_from(slot)
-        prhs[0:FEATS, :] = hrecv[slot, 0:FEATS, :]
-        weights = hrecv[slot, FEATS:PAY, :]
-        for i in range(FEATS // 16):
-            prhs[FEATS + 16 * i:FEATS + 16 * (i + 1), :] = weights
-        hits = jnp.where(node == rrows[pl.ds(source, 1), :], 1.0, 0.0).astype(BF16)
-        acc[...] += lax.dot_general(hits, prhs[...], (((1,), (1,)), ((), ())), preferred_element_type=F32)
-
-    def take_halos(lo, hi):
-        def body(slot, _):
-            halo_copy(slot).wait_recv()
-            take_halo(slot)
-            return 0
-        lax.fori_loop(lo, hi, body, 0)
+    def take_halo(*slots):
+        for slot in slots:
+            if slot != 8:
+                halo_copy(slot).wait_recv()
+        hits = jnp.concatenate(
+            [jnp.where(node == rrows[pl.ds(halo_from(slot), 1), :], 1.0, 0.0).astype(BF16) for slot in slots], axis=1
+        )
+        rows = jnp.concatenate([hrecv[slot] for slot in slots], axis=1)
+        acc[:, 0:PAY] += lax.dot_general(hits, rows, (((1,), (1,)), ((), ())), preferred_element_type=F32)
 
     pl.semaphore_wait(barrier, 11)
 
@@ -272,12 +266,12 @@
     landed(1, 0)
     absorb(1, side)
     build_halo(fxt, prows, pweight, halo_to(0), hrecv.at[8])
-    take_halo(8)
     landed(6, 1)
     send(6, 10, 1, up)
     landed(7, 1)
     send(7, 11, 1, down)
     absorb_pair(6, 2, xl)
+    take_halo(1, 2)
     landed(10, 0)
     send(10, 14, 0, up)
     send(10, 12, 0, side)
@@ -286,31 +280,35 @@
     landed(4, 0)
     landed(5, 0)
     absorb_pair(4, 1, other)
+    take_halo(3, 4)
     landed(8, 1)
     send(8, 12, 1, up)
     landed(9, 1)
     send(9, 13, 1, down)
-    take_halos(1, 5)
+    take_halo(5, 6)
+    take_halo(7, 8)
     landed(10, 1)
     landed(11, 1)
     send(11, 14, 1, down)
     absorb_pair(10, 3, xl)
+    take_halo(9, 10)
     landed(14, 0)
     send(14, 15, 0, side)
     landed(8, 0)
     landed(9, 0)
     absorb_pair(8, 2, other)
+    take_halo(11, 12)
     landed(12, 1)
     send(12, 15, 2, up)
     landed(13, 1)
     send(13, 15, 3, down)
     landed(14, 1)
     absorb(14, xl * NZ + lax.rem(z + 4, NZ))
-    take_halos(5, 8)
-    take_halos(9, 16)
+    take_halo(13, 14)
     landed(12, 0)
     landed(13, 0)
     absorb_pair(12, 3, other)
+    take_halo(15)
     landed(15, 2)
     landed(15, 3)
     landed(15, 0)
@@ -324,7 +322,7 @@
     total_w = jnp.zeros((FEATS, 2 * FEATS), F32)
     for r in range(4):
         rs = pl.ds(r * TILE, TILE)
-        total = 1.0 + acc[rs, FEATS:] + jnp.broadcast_to(degree[:, r:r + 1], (TILE, FEATS))
+        total = jnp.broadcast_to(1.0 + acc[rs, FEATS:FEATS + 1] + degree[:, r:r + 1], (TILE, FEATS))
         agg = (acc[rs, 0:FEATS] * lax.rsqrt(total)).astype(BF16)
         cat = jnp.concatenate([part[0, rs, :], agg], axis=1)
         pre = jnp.dot(cat, wcat, preferred_element_type=F32) + bias_row
@@ -432,7 +430,6 @@
             pltpu.VMEM((FEATS, ROWS), BF16),
             pltpu.VMEM((16, PAY, HALO), BF16),
             pltpu.VMEM((16, PAY, HALO), BF16),
-            pltpu.VMEM((2 * FEATS, HALO), BF16),
             pltpu.VMEM((16, 24, FEATS), F32),
             pltpu.VMEM((16, 24, FEATS), F32),
             pltpu.VMEM((16, 8, FEATS), F32),

time: 47.1 us -> 46 us (0.977)
  Pallas kernels: 44.6 us -> 43.5 us
    pallas_call x1, Pallas kernels: 44.6 us -> 43.5 us  [local(): pl.pallas_call(kernel, out_shape=(jax.ShapeDtypeStruct((ROWS, FEATS), BF1...]
where the time goes in v4:
time: 46 us; the launch traced here: 45.9 us
  Pallas kernels  43.5 us (95%)
  local copies, waits for them, and re-layouts  1.76 us (4%)
  between operations  0.64 us (1%)
    pallas_call x1, Pallas kernels, local(): pl.pallas_call(kernel, out_shape=(jax.ShapeDtypeStruct((ROWS, FEATS), BF1...  43.5 us
    unnamed x3, local copies, waits for them, and re-layouts  1.76 us

profile of v4, /device:TPU:1, one launch (start us, length us, event | category | flops | bytes accessed | tf_op | source)
XLA Modules:
  0.0 45.9 jit_solution(9915184358346280130)
XLA Ops:
  0.6 43.5 %shard_map.148 = (bf16[512,128]{1,0:T(8,128)(2,1)S(1)}, f32[8,16]{1,0:T(8,128)S(1)}, f32[1,128]{1,0:T(1,128)S(1)}) custom-call(bf16[512,128]{1,0:T(8,128)(2,1)} %bitcast.22, bf16[16,8,128,128]{3,2,1,0:T(8,128)(2,1)} %bitcast.21, bf16[512,128]{1,0:T(8,128)(2,1)} %bitcast.23, bf16[128,128]{1,0:T(8,128)(2,1)} %wself_in.1, bf16[128,128]{1,0:T(8,128)(2,1)} %wneigh_in.1, ...), custom_call_target="tpu_custom_call" | custom-call | tf_op jit(solution)/shard_map/pallas_call | solution.py:405
  44.1 0.7 %copy.19 = bf16[1,1,512,128]{3,2,1,0:T(8,128)(2,1)} copy(bf16[1,1,512,128]{3,2,1,0:T(8,128)(2,1)S(1)} %bitcast.18) | data formatting | bytes 262144
  44.8 0.6 %copy.20 = f32[16,8]{0,1:T(8,128)} copy(f32[16,8]{0,1:T(8,128)S(1)} %bitcast.19) | data formatting | bytes 1024
  45.4 0.5 %copy.21 = f32[128]{0:T(128)} copy(f32[128]{0:T(128)S(1)} %bitcast.20) | data formatting | bytes 1024

commit v5 on v4

--- a/solution.py
+++ b/solution.py
@@ -9,7 +9,7 @@
 
 MESH = pl.DeviceIdType.MESH
 ROWS, FEATS, TILE, SLOTS, HALO = 512, 128, 128, 8, 256
-HALF = ROWS // 2
+SPLIT = 320
 NZ = 8
 PAY = FEATS + 16
 BF16, F32 = jnp.bfloat16, jnp.float32
@@ -27,7 +27,8 @@
 
 DOM_FAR = sorted(range(1, 16), key=lambda j: -dom_hops(j))
 GRP_FAR = sorted(range(1, 16), key=lambda j: -grp_hops(j))
-PIECES = ((0, HALF), (HALF, HALF), (HALF, HALF // 2), (HALF + HALF // 2, HALF // 2))
+REST = ROWS - SPLIT
+PIECES = ((0, SPLIT), (SPLIT, REST), (SPLIT, REST // 2), (SPLIT + REST // 2, REST // 2))
 
 
 def kernel(
@@ -228,9 +229,9 @@
     other = 1 - xl
     landed(2, 0)
     send(2, 6, 0, up)
-    send(2, 4, 0, side)
     landed(3, 0)
     send(3, 7, 0, down)
+    send(2, 4, 0, side)
     send(3, 5, 0, side)
     landed(1, 1)
     send(1, 4, 1, up)
@@ -254,9 +255,9 @@
 
     landed(6, 0)
     send(6, 10, 0, up)
-    send(6, 8, 0, side)
     landed(7, 0)
     send(7, 11, 0, down)
+    send(6, 8, 0, side)
     send(7, 9, 0, side)
     absorb_pair(2, 1, xl)
     landed(4, 1)

time: 46 us -> 45.6 us (level)
  no operation moved by 1% of the time
where the time goes in v5:
time: 45.6 us; the launch traced here: 45.5 us
  Pallas kernels  43.1 us (95%)
  local copies, waits for them, and re-layouts  1.76 us (4%)
  between operations  0.64 us (1%)
    pallas_call x1, Pallas kernels, local(): pl.pallas_call(kernel, out_shape=(jax.ShapeDtypeStruct((ROWS, FEATS), BF1...  43.1 us
    unnamed x3, local copies, waits for them, and re-layouts  1.76 us

profile of v5, /device:TPU:1, one launch (start us, length us, event | category | flops | bytes accessed | tf_op | source)
XLA Modules:
  0.0 45.5 jit_solution(16686598137780447275)
XLA Ops:
  0.6 43.1 %shard_map.148 = (bf16[512,128]{1,0:T(8,128)(2,1)S(1)}, f32[8,16]{1,0:T(8,128)S(1)}, f32[1,128]{1,0:T(1,128)S(1)}) custom-call(bf16[512,128]{1,0:T(8,128)(2,1)} %bitcast.22, bf16[16,8,128,128]{3,2,1,0:T(8,128)(2,1)} %bitcast.21, bf16[512,128]{1,0:T(8,128)(2,1)} %bitcast.23, bf16[128,128]{1,0:T(8,128)(2,1)} %wself_in.1, bf16[128,128]{1,0:T(8,128)(2,1)} %wneigh_in.1, ...), custom_call_target="tpu_custom_call" | custom-call | tf_op jit(solution)/shard_map/pallas_call | solution.py:406
  43.8 0.7 %copy.19 = bf16[1,1,512,128]{3,2,1,0:T(8,128)(2,1)} copy(bf16[1,1,512,128]{3,2,1,0:T(8,128)(2,1)S(1)} %bitcast.18) | data formatting | bytes 262144
  44.4 0.6 %copy.20 = f32[16,8]{0,1:T(8,128)} copy(f32[16,8]{0,1:T(8,128)S(1)} %bitcast.19) | data formatting | bytes 1024
  45.0 0.5 %copy.21 = f32[128]{0:T(128)} copy(f32[128]{0:T(128)S(1)} %bitcast.20) | data formatting | bytes 1024
